TPU v7x, 128 devices: a whole 4x4x4 slice. The times are simulated.
128 devices in a mesh: dp: 32 (over x, z, core), mp: 4 (over y).
Axes of the slice: x: 4, y: 4, z: 4, core: 2. Of those that a mesh axis runs over, the one named last changes fastest.
Arguments:
- delays: float32 [262144], P('dp'), may hold values from -6 to 6
- kernel_tiles: bfloat16 [32, 4, 256, 128, 128], P('dp', 'mp'), may hold values from -0.09375 to 0.09375
- row_blocks: int32 [32, 4, 256], P('dp', 'mp'), may hold values from 0 to 63
- col_blocks: int32 [32, 4, 256], P('dp', 'mp'), may hold values from 0 to 4095
- tile_counts: int32 [32, 4], P('dp', 'mp'), may hold values from 64 to 256, as said below
Outputs:
- slowness: float32 [2097152], P('mp')
- left_dir: float32 [262144], P('dp')
Inputs may be any that keep to these rules, and one draw needn't show every extreme that they name: tile_counts[d, m] is the number of leading live tile slots of device (d, m); some device is full in every draw.
All inputs are finite; a program needn't handle non-finite values.
Results may differ from a plain program's by a relative error of at most 0.0076.
Values sent between devices are 32-bit elements; how exact they have to be, the bound alone decides.
A program may use at most 64 MiB of HBM per device.

v0:
```python
from functools import partial

import jax
import jax.numpy as jnp
from jax import lax
from jax.sharding import PartitionSpec as P

CB_DEV = 4096
ITERS = 2


norm_eps = 1e-06


def forward_block(tiles_blk, rows_blk, cols_blk, live, right_low, row_count):
    picked = jnp.take(right_low, cols_blk, axis=0)
    products = jnp.einsum("kij,kj->ki", tiles_blk, picked, preferred_element_type=jnp.float32)
    chooser = (
        (rows_blk[:, None] == jnp.arange(row_count, dtype=jnp.int32)[None, :]) & live[:, None]
    ).astype(jnp.float32)
    return jnp.dot(
        chooser.T, products, precision=lax.Precision.HIGHEST, preferred_element_type=jnp.float32
    )


def backward_block(tiles_blk, rows_blk, cols_blk, live, left_low, cell_count):
    picked = jnp.take(left_low, rows_blk, axis=0)
    products = jnp.einsum("kij,ki->kj", tiles_blk, picked, preferred_element_type=jnp.float32)
    products = products * live[:, None].astype(jnp.float32)
    return jax.ops.segment_sum(products, cols_blk, num_segments=cell_count)


def run_tiles(kernel, rows_all, cols_all, live_count, block_fn):
    slot_total = kernel.shape[0]
    live = jnp.arange(slot_total, dtype=jnp.int32) < live_count
    return block_fn(kernel, rows_all, cols_all, live)


def beta_total(partial_sq):
    return lax.psum(partial_sq, "dp")


def shards(delays, kernel_tiles, row_blocks, col_blocks, tile_counts):
    kernel = kernel_tiles[0, 0]
    rows_all = row_blocks[0, 0]
    cols_all = col_blocks[0, 0]
    live_count = tile_counts[0, 0]
    tile_size = kernel.shape[1]
    row_count = delays.shape[0] // tile_size
    cell_count = CB_DEV
    delays_mat = delays.reshape(row_count, tile_size)

    def backward_local(left_raw):
        block_fn = partial(
            backward_block, left_low=left_raw.astype(jnp.bfloat16), cell_count=cell_count
        )
        return run_tiles(kernel, rows_all, cols_all, live_count, block_fn)

    def model_combine(back_partial, left_raw, right_dir):
        partial_sq = jnp.sum(left_raw * left_raw)
        beta_sq = beta_total(partial_sq)
        total = lax.psum(back_partial, "dp")
        beta_now = jnp.sqrt(beta_sq + norm_eps)
        right_raw = total / beta_now
        if right_dir is not None:
            right_raw = right_raw - beta_now * right_dir
        return (right_raw, beta_now)

    right_raw, beta_now = model_combine(backward_local(delays_mat), delays_mat, None)
    left_dir = delays_mat / beta_now
    phi_bar = beta_now
    slowness = jnp.zeros((cell_count, tile_size), jnp.float32)
    search_dir = slowness
    rho_now = beta_now
    cosine = beta_now
    sine_val = beta_now
    for iteration in range(ITERS):
        forward_block_fn = partial(
            forward_block, right_low=right_raw.astype(jnp.bfloat16), row_count=row_count
        )
        partial_rows = run_tiles(kernel, rows_all, cols_all, live_count, forward_block_fn)
        data_partial_sq = jnp.sum(right_raw * right_raw)
        alpha_sq = lax.psum(data_partial_sq, "mp")
        image = lax.psum(partial_rows, "mp")
        image, alpha_sq = (image, alpha_sq)
        alpha_now = jnp.sqrt(alpha_sq + norm_eps)
        right_dir = right_raw / alpha_now
        if iteration == 0:
            search_dir = right_dir
            rho_bar = alpha_now
        else:
            theta_now = sine_val * alpha_now
            rho_bar = -cosine * alpha_now
            search_dir = right_dir - theta_now / rho_now * search_dir
        left_raw = image / alpha_now - alpha_now * left_dir
        if iteration + 1 < ITERS:
            right_raw, beta_now = model_combine(backward_local(left_raw), left_raw, right_dir)
        else:
            beta_now = jnp.sqrt(beta_total(jnp.sum(left_raw * left_raw)) + norm_eps)
        left_dir = left_raw / beta_now
        rho_now = jnp.sqrt(rho_bar * rho_bar + beta_now * beta_now)
        cosine = rho_bar / rho_now
        sine_val = beta_now / rho_now
        phi_now = cosine * phi_bar
        phi_bar = sine_val * phi_bar
        slowness = slowness + phi_now / rho_now * search_dir
    return (slowness.reshape(-1), left_dir.reshape(-1))


def solution(mesh):
    in_specs = (
        P("dp"),
        P("dp", "mp", None, None, None),
        P("dp", "mp", None),
        P("dp", "mp", None),
        P("dp", "mp"),
    )
    out_specs = (P("mp"), P("dp"))
    return jax.shard_map(shards, mesh=mesh, in_specs=in_specs, out_specs=out_specs, check_vma=False)
```

profile of v0, /device:TPU:1, one launch (start us, length us, event | category | flops | bytes accessed | tf_op | source)
XLA Modules:
  0.0 385.5 jit_solution(16990409059721446217)
XLA Ops:
  7.2 0.0 all-reduce.5.cloned.1.call-start
  7.2 0.7 compare_select_fusion.1
  7.9 0.7 compare_and_fusion.1
  8.6 1.4 multiply_reduce_fusion.4
  10.7 0.9 gather_fusion
  11.6 0.1 select_bitcast_fusion.3
  11.7 0.0 copy-start.4
  11.7 5.7 %fusion.6 = f32[256,1,128]{2,1,0:T(1,128)S(1)} fusion(bf16[1,1,256,128,128]{4,3,2,1,0:T(8,128)(2,1)} %param.10, bf16[256,128,1]{1,0,2:T(8,128)(2,1)S(1)} %select_bitcast_fusion.3), kind=kOutput, calls=%fused_computation.12 | convolution fusion | flops 8388608 | bytes 8585216 | tf_op jit(solution)/shard_map/kij,ki->kj/dot_general | solution.py:28
  17.3 0.0 copy-done.4
  17.3 2.9 scatter_custom_fusion
  20.3 0.0 all-reduce.5.cloned.1.call-update
  20.3 0.0 all-reduce.7.cloned.1.call-start
  20.3 65.6 %psum.64 = f32[]{:T(128)} all-reduce(f32[]{:T(128)} %get-tuple-element.16), channel_id=1, replica_groups=mesh['dp'=32,'mp'=4] {'dp'}, use_global_device_ids=true, to_apply=%region_3.5 | all-reduce | flops 1 | bytes 8 | tf_op jit(solution)/shard_map/psum | solution.py:40
  86.7 44.4 %all-reduce.5.cloned.1.call-done = f32[4096,128]{1,0:T(8,128)} async-done(((f32[4096,128]{1,0:T(8,128)}), f32[4096,128]{1,0:T(8,128)}) %all-reduce.5.cloned.1.call-update) | async-done | bytes 2097168 | tf_op jit(solution)/shard_map/psum | solution.py:62
  131.1 2.7 multiply_reduce_fusion.1
  133.8 0.9 gather_fusion.1
  134.7 0.1 select_bitcast_fusion.2
  134.8 0.0 copy-start.3
  134.8 0.0 copy-start.2
  134.8 7.8 %fusion.4 = f32[256,1,128]{2,1,0:T(1,128)S(1)} fusion(bf16[1,1,256,128,128]{4,3,2,1,0:T(8,128)(2,1)} %param.10, bf16[256,128,1]{1,0,2:T(8,128)(2,1)S(1)} %select_bitcast_fusion.2), kind=kOutput, calls=%fused_computation.10 | convolution fusion | flops 8388608 | bytes 8585216 | tf_op jit(solution)/shard_map/kij,kj->ki/dot_general | solution.py:17
  142.6 0.0 copy-done.3
  142.6 0.4 fusion.22
  143.0 14.6 %all-reduce.1 = (f32[64,128]{1,0:T(8,128)S(1)}, f32[]{:T(128)}) all-reduce(f32[64,128]{1,0:T(8,128)S(1)} %fusion.22, f32[]{:T(128)} %get-tuple-element.14), channel_id=1, replica_groups=mesh['dp'=32,'mp'=4] {'mp'}, use_global_device_ids=true, to_apply=%region_6.9 | all-reduce | flops 8193 | bytes 65544 | tf_op jit(solution)/shard_map/psum | solution.py:84
  158.3 0.0 copy-done.2
  158.3 0.6 multiply_reduce_fusion.3
  158.9 0.9 gather_fusion.2
  159.8 0.1 select_bitcast_fusion.1
  159.9 5.7 %fusion.2 = f32[256,1,128]{2,1,0:T(1,128)S(1)} fusion(bf16[1,1,256,128,128]{4,3,2,1,0:T(8,128)(2,1)} %param.10, bf16[256,128,1]{1,0,2:T(8,128)(2,1)S(1)} %select_bitcast_fusion.1), kind=kOutput, calls=%fused_computation.8 | convolution fusion | flops 8388608 | bytes 8585216 | tf_op jit(solution)/shard_map/kij,ki->kj/dot_general | solution.py:28
  165.5 0.0 copy-start
  165.5 2.9 scatter_custom_fusion.1
  168.5 0.0 all-reduce.7.cloned.1.call-update
  168.5 67.5 %psum.67 = f32[]{:T(128)} all-reduce(f32[]{:T(128)} %get-tuple-element.12), channel_id=1, replica_groups=mesh['dp'=32,'mp'=4] {'dp'}, use_global_device_ids=true, to_apply=%region_8.11 | all-reduce | flops 1 | bytes 8 | tf_op jit(solution)/shard_map/psum | solution.py:40
  236.8 40.3 %all-reduce.7.cloned.1.call-done = f32[4096,128]{1,0:T(8,128)} async-done(((f32[4096,128]{1,0:T(8,128)}), f32[4096,128]{1,0:T(8,128)}) %all-reduce.7.cloned.1.call-update) | async-done | bytes 2097168 | tf_op jit(solution)/shard_map/psum | solution.py:62
  277.1 0.0 copy-done
  277.1 3.3 fusion.31
  280.4 0.9 gather_fusion.3
  281.3 0.1 select_bitcast_fusion
  281.4 0.0 copy-start.1
  281.4 7.9 %fusion = f32[256,1,128]{2,1,0:T(1,128)S(1)} fusion(bf16[1,1,256,128,128]{4,3,2,1,0:T(8,128)(2,1)} %param.10, bf16[256,128,1]{1,0,2:T(8,128)(2,1)S(1)} %select_bitcast_fusion), kind=kOutput, calls=%fused_computation.6 | convolution fusion | flops 8388608 | bytes 8585216 | tf_op jit(solution)/shard_map/kij,kj->ki/dot_general | solution.py:17
  289.3 0.4 fusion.20
  289.7 0.0 copy-done.1
  289.7 1.1 multiply_reduce_fusion
  290.9 14.5 %all-reduce = (f32[]{:T(128)}, f32[64,128]{1,0:T(8,128)S(1)}) all-reduce(f32[]{:T(128)} %multiply_reduce_fusion, f32[64,128]{1,0:T(8,128)S(1)} %fusion.20), channel_id=1, replica_groups=mesh['dp'=32,'mp'=4] {'mp'}, use_global_device_ids=true, to_apply=%region_12.15 | all-reduce | flops 8193 | bytes 65544 | tf_op jit(solution)/shard_map/psum | solution.py:83
  306.1 0.6 multiply_reduce_fusion.2
  306.7 67.1 %psum.71 = f32[]{:T(128)} all-reduce(f32[]{:T(128)} %get-tuple-element.8), channel_id=1, replica_groups=mesh['dp'=32,'mp'=4] {'dp'}, use_global_device_ids=true, to_apply=%region_15.18 | all-reduce | flops 1 | bytes 8 | tf_op jit(solution)/shard_map/psum | solution.py:40
  374.5 0.6 divide_bitcast_fusion
  375.3 3.4 add_bitcast_fusion
  (7 shorter events, 0.0 us)
Async XLA Ops:
  7.2 123.9 %all-reduce.5.cloned.1.call-start = ((), (), s32[]{:S(2)}) async-start(), calls=%async_computation | async-start | bytes 4194304 | tf_op jit(solution)/shard_map/psum | solution.py:62
  11.7 5.7 %copy-start.4 = (s32[1,1,256]{2,1,0:T(1,128)S(1)}, s32[1,1,256]{2,1,0:T(1,128)}, u32[]{:S(2)}) copy-start(s32[1,1,256]{2,1,0:T(1,128)} %param.12) | copy-start | bytes 3076
  20.3 256.8 %all-reduce.7.cloned.1.call-start = ((), (), s32[]{:S(2)}) async-start(), calls=%async_computation.1 | async-start | bytes 4194304 | tf_op jit(solution)/shard_map/psum | solution.py:62
  134.8 7.8 %copy-start.3 = (s32[1,1,256]{2,1,0:T(1,128)S(1)}, s32[1,1,256]{2,1,0:T(1,128)}, u32[]{:S(2)}) copy-start(s32[1,1,256]{2,1,0:T(1,128)} %param.11) | copy-start | bytes 3076
  134.8 23.5 %copy-start.2 = (f32[8192]{0:T(1024)S(1)}, f32[8192]{0:T(1024)}, u32[]{:S(2)}) copy-start(f32[8192]{0:T(1024)} %param.9) | copy-start | bytes 98308
  165.5 111.6 %copy-start = (f32[4096,128]{1,0:T(8,128)S(1)}, f32[4096,128]{1,0:T(8,128)}, u32[]{:S(2)}) copy-start(f32[4096,128]{1,0:T(8,128)} %all-reduce.5.cloned.1.call-done) | copy-start | bytes 6291460
  281.4 8.3 %copy-start.1 = (f32[4096,128]{1,0:T(8,128)S(1)}, f32[4096,128]{1,0:T(8,128)}, u32[]{:S(2)}) copy-start(f32[4096,128]{1,0:T(8,128)} %get-tuple-element.11) | copy-start | bytes 6291460
Sparse Core Ops, SparseCore 0:
  20.4 110.6 all-reduce.4
  168.6 108.4 all-reduce.6
where the time goes:
time: 386 us
  blocking collectives  229 us (59%)
  waiting for transfers between devices  84.7 us (22%)
  matrix products  27.8 us (7%)
  other arithmetic  21.6 us (6%)
  between operations  18.6 us (5%)
    psum x3, blocking collectives, beta_total(): return lax.psum(partial_sq, 'dp')  200 us
    psum x2, waiting for transfers between devices, model_combine(): total = lax.psum(back_partial, 'dp')  84.7 us
    dot_general x2, matrix products, forward_block(): jnp.einsum('kij,kj->ki', tiles_blk, picked, preferred_element_type=jnp.fl...  15.7 us
    psum x1, blocking collectives, shards(): image = lax.psum(partial_rows, 'mp')  14.6 us
    psum x1, blocking collectives, shards(): alpha_sq = lax.psum(data_partial_sq, 'mp')  14.5 us
    dot_general x2, matrix products, backward_block(): jnp.einsum('kij,ki->kj', tiles_blk, picked, preferred_element_type=jnp.fl...  11.3 us
  transfers between devices with their start and end apart: 2, of which 2 were waited for; matrix products, arithmetic and copies ran while one was open for 0% of the time, Pallas kernels for 0%

commit v1 on v0

v1 whole, which is shorter than its diff:
```python
import jax
import jax.numpy as jnp
from jax import lax
from jax.experimental import pallas as pl
from jax.experimental.pallas import tpu as pltpu
from jax.sharding import PartitionSpec as P

TILE = 128
SLOTS = 256
HALF = SLOTS // 2
ROW_BLOCKS = 64
CELL_BLOCKS = 4096
CHUNK = CELL_BLOCKS // 32
PAIR_ROWS = SLOTS + CHUNK
BLOCK_ROWS = HALF + 8
GROUP = 8
LOAD_CHUNKS = 8
norm_eps = 1e-06

MESH = pl.DeviceIdType.MESH
F32 = jnp.float32
BF16 = jnp.bfloat16
NT = (((1,), (1,)), ((), ()))

SIDES = (1, 3, 2)


def split_parts(values):
    high = values.astype(BF16)
    low = (values - high.astype(F32)).astype(BF16)
    return high, low


def side_by_side(values):
    return jnp.concatenate(split_parts(values), axis=1)


def total_of(values):
    return jnp.sum(jnp.sum(values, axis=0, keepdims=True), axis=1, keepdims=True)


def tree4(parts):
    return (parts[0] + parts[2]) + (parts[1] + parts[3])


def lsqr_kernel(
    count_ref,
    delays_ref,
    rows_ref,
    cols_ref,
    tiles_hbm,
    slow_hbm,
    left_ref,
    tiles,
    picked,
    slot_products,
    gather_first,
    gather_second,
    targets,
    row_pick,
    row_sum,
    summed,
    cols_out,
    cols_in,
    pair_out,
    pair_in,
    image_out,
    image_in,
    norm_out,
    norm_in,
    dense_first,
    dense_second,
    slow_buf,
    load_sem,
    store_sem,
    gather_send,
    gather_recv,
    cols_sem,
    pair_sem,
    image_send,
    image_recv,
    norm_send,
    norm_recv,
    dense_send,
    dense_recv,
):
    dp = lax.axis_index("dp")
    mp = lax.axis_index("mp")
    at_x, at_z, core = dp // 8, (dp // 2) % 4, dp % 2

    def peer(off_x, off_z, off_core=0, off_y=0):
        there = ((at_x + off_x) % 4) * 8 + ((at_z + off_z) % 4) * 2 + (core + off_core) % 2
        return (there, (mp + off_y) % 4)

    sibling = peer(0, 0, 1)

    def remote(src, dst, send, recv, device):
        return pltpu.make_async_remote_copy(
            src_ref=src, dst_ref=dst, send_sem=send, recv_sem=recv, device_id=device, device_id_type=MESH
        )

    loads = []
    load_rows = SLOTS * TILE // LOAD_CHUNKS
    for part in range(LOAD_CHUNKS):
        span = pl.ds(part * load_rows, load_rows)
        load = pltpu.make_async_copy(tiles_hbm.at[span], tiles.at[span], load_sem.at[part])
        load.start()
        loads.append(load)

    barrier = pltpu.get_barrier_semaphore()
    partners = [peer(side, 0) for side in SIDES] + [peer(0, side) for side in SIDES]
    partners += [sibling] + [peer(0, 0, 0, side) for side in SIDES]
    for partner in partners:
        pl.semaphore_signal(barrier, inc=1, device_id=partner, device_id_type=MESH)

    sent = []

    count = count_ref[0, 0]
    rows_f = rows_ref[...].astype(F32)
    cols_f = cols_ref[...].astype(F32)
    lane_f = lax.broadcasted_iota(jnp.int32, (TILE, TILE), 1).astype(F32)
    sub_i = lax.broadcasted_iota(jnp.int32, (TILE, TILE), 0)
    for half in range(2):
        down = jnp.transpose(jnp.broadcast_to(rows_f[half : half + 1, :], (TILE, TILE)))
        live = sub_i + half * HALF < count
        row_pick[pl.ds(half * HALF, HALF), :] = jnp.where((down == lane_f) & live, 1.0, 0.0).astype(BF16)
        across = jnp.broadcast_to(rows_f[half : half + 1, :], (ROW_BLOCKS, TILE))
        sub_r = lax.broadcasted_iota(jnp.int32, (ROW_BLOCKS, TILE), 0).astype(F32)
        lane_r = lax.broadcasted_iota(jnp.int32, (ROW_BLOCKS, TILE), 1) + half * HALF
        row_sum[:, pl.ds(half * HALF, HALF)] = jnp.where((across == sub_r) & (lane_r < count), 1.0, 0.0).astype(BF16)
        targets[pl.ds(half * HALF, HALF), :] = jnp.transpose(
            jnp.broadcast_to(cols_f[half : half + 1, :], (TILE, TILE))
        )
    first_block = ((dp // 2) * (2 * CHUNK)).astype(F32)
    core_f = core.astype(F32)
    chunk_f = sub_i.astype(F32) + first_block
    targets[pl.ds(SLOTS, CHUNK), :] = chunk_f + core_f * CHUNK
    targets[pl.ds(PAIR_ROWS + SLOTS, CHUNK), :] = chunk_f + (1.0 - core_f) * CHUNK
    cols_out[...] = jnp.concatenate([cols_f, jnp.zeros((6, TILE), F32)], axis=0)

    def pick_rows(vector):
        padded = jnp.concatenate([vector, jnp.zeros((TILE - ROW_BLOCKS, TILE), F32)], axis=0)
        picked[...] = jnp.dot(row_pick[...], side_by_side(padded), preferred_element_type=F32)

    row_in_group = lax.broadcasted_iota(jnp.int32, (2 * GROUP, TILE), 0) % GROUP
    sub_group = lax.broadcasted_iota(jnp.int32, (GROUP, TILE), 0)

    def both_parts(group):
        span = pl.ds(group * GROUP, GROUP)
        return jnp.concatenate([picked[span, pl.ds(0, TILE)], picked[span, pl.ds(TILE, TILE)]], axis=0)

    def back_group(group, block, first):
        parts = both_parts(group)
        lhs = jnp.concatenate(
            [jnp.where(row_in_group == slot, parts, 0.0).astype(BF16) for slot in range(GROUP)], axis=1
        )
        weights = tiles[pl.ds(group * (GROUP * TILE), GROUP * TILE), :]
        out = jnp.dot(lhs, weights, preferred_element_type=F32)
        block[pl.ds((group - first) * GROUP, GROUP), :] = out[:GROUP] + out[GROUP:]

    def forward_group(group):
        lhs = both_parts(group).astype(BF16)
        weights = tiles[pl.ds(group * (GROUP * TILE), GROUP * TILE), :]
        out = lax.dot_general(lhs, weights, NT, preferred_element_type=F32)
        out = out[:GROUP] + out[GROUP:]
        chosen = out[:, :TILE]
        for slot in range(1, GROUP):
            chosen = jnp.where(sub_group == slot, out[:, slot * TILE : (slot + 1) * TILE], chosen)
        slot_products[pl.ds(group * GROUP, GROUP), :] = chosen

    def forward(right):
        high, low = split_parts(right)
        picked[:, pl.ds(0, TILE)] = high.astype(F32)
        picked[:, pl.ds(TILE, TILE)] = low.astype(F32)

        @pl.loop(0, SLOTS // GROUP, unroll=4)
        def _(group):
            forward_group(group)

        out = jnp.dot(row_sum[...], side_by_side(slot_products[...]), preferred_element_type=F32)
        return out[:, :TILE] + out[:, TILE:]

    def scalar_rows(scalars):
        rows = [jnp.broadcast_to(value, (1, TILE)) for value in scalars]
        rows = [jnp.zeros((1, TILE), F32)] + rows
        rows += [jnp.zeros((8 - len(rows), TILE), F32)]
        return jnp.concatenate(rows, axis=0)

    def back_and_gather(step, gathered, scalars, waits):
        def arrival(half, off_x, off_z):
            block = gathered.at[half, off_x, off_z]
            return remote(
                block, block, gather_send.at[step, half, off_x, off_z], gather_recv.at[step, half, off_x, off_z], sibling
            )

        def send(half, off_x, off_z, side, along_x):
            to_x, to_z = (off_x - side) % 4, (off_z - side) % 4
            dst = (to_x, off_z) if along_x else (off_x, to_z)
            device = peer(side, 0) if along_x else peer(0, side)
            copy = remote(
                gathered.at[half, off_x, off_z],
                gathered.at[half, dst[0], dst[1]],
                gather_send.at[step, half, dst[0], dst[1]],
                gather_recv.at[step, half, dst[0], dst[1]],
                device,
            )
            copy.start()
            sent.append(copy)

        chunks = LOAD_CHUNKS // 2
        groups = HALF // GROUP
        for half in range(2):
            tail = scalar_rows(scalars)
            lane_cols = jnp.broadcast_to(cols_f[half : half + 1, :], (8, TILE))
            own = gathered.at[half, 0, 0]
            own[pl.ds(HALF, 8), :] = jnp.where(sub_group == 0, lane_cols, tail)
            for part in range(chunks):
                if waits:
                    loads[half * chunks + part].wait()
                per = groups // chunks
                start = half * groups + part * per

                @pl.loop(0, per, unroll=per)
                def _(index):
                    back_group(start + index, own, half * groups)

            if waits and half == 0:
                pl.semaphore_wait(barrier, len(partners))
                swap = remote(cols_out, cols_in, cols_sem.at[0], cols_sem.at[1], sibling)
                swap.start()
                sent.append(swap)
            for side in SIDES:
                send(half, 0, 0, side, half == 0)
        for half in range(2):
            for side in SIDES:
                send(half, 0, 0, side, half == 1)
        if waits:
            swap.wait_recv()
            other = cols_in[...]
            for half in range(2):
                targets[pl.ds(PAIR_ROWS + half * HALF, HALF), :] = jnp.transpose(
                    jnp.broadcast_to(other[half : half + 1, :], (TILE, TILE))
                )
        for off in (3, 1, 2):
            arrival(0, off, 0).wait_recv()
            for side in SIDES:
                send(0, off, 0, side, False)
            arrival(1, 0, off).wait_recv()
            for side in SIDES:
                send(1, 0, off, side, True)

        order = [(0, 0)] + [(off, 0) for off in (3, 1, 2)] + [(0, off) for off in (3, 1, 2)]
        order += [(off_x, off_z) for off_z in (3, 1, 2) for off_x in (3, 1, 2)]
        for number, (off_x, off_z) in enumerate(order):
            if off_z:
                if off_x or not off_x:
                    pass
            if off_z != 0:
                arrival(0, off_x, off_z).wait_recv()
            if off_x != 0:
                arrival(1, off_x, off_z).wait_recv()
            values = jnp.concatenate(
                [
                    side_by_side(gathered[0, off_x, off_z, pl.ds(0, HALF), :]),
                    side_by_side(gathered[1, off_x, off_z, pl.ds(0, HALF), :]),
                ],
                axis=0,
            )
            ids = [gathered[half, off_x, off_z, pl.ds(HALF, 1), :] for half in range(2)]

            @pl.loop(0, 2 * PAIR_ROWS // 256)
            def _(part):
                span = pl.ds(part * 256, 256)
                want = targets[span, :]
                hits = jnp.concatenate([jnp.where(want == one, 1.0, 0.0).astype(BF16) for one in ids], axis=1)
                out = jnp.dot(hits, values, preferred_element_type=F32)
                if number == 0:
                    summed[span, :] = out
                else:
                    summed[span, :] = summed[span, :] + out

        scalar_tree = tree4(
            [tree4([gathered[0, off_x, off_z, pl.ds(HALF, 8), :] for off_x in range(4)]) for off_z in range(4)]
        )
        other_half = summed[pl.ds(PAIR_ROWS, PAIR_ROWS), :]
        pair_out[step, pl.ds(0, PAIR_ROWS), :] = other_half[:, :TILE] + other_half[:, TILE:]
        pair_out[step, pl.ds(PAIR_ROWS, 8), :] = scalar_tree
        swap_sums = remote(
            pair_out.at[step], pair_in.at[step], pair_sem.at[step, 0], pair_sem.at[step, 1], sibling
        )
        swap_sums.start()
        sent.append(swap_sums)
        mine = summed[pl.ds(0, PAIR_ROWS), :]
        mine = mine[:, :TILE] + mine[:, TILE:]
        swap_sums.wait_recv()
        mine = mine + pair_in[step, pl.ds(0, PAIR_ROWS), :]
        sums = scalar_tree + pair_in[step, pl.ds(PAIR_ROWS, 8), :]
        return mine, sums

    def dense_one(step, dense, chunk):
        dense[at_x, at_z, core] = chunk
        for along in range(2):
            for side in SIDES:
                span = pl.ds(along * (CHUNK // 2), CHUNK // 2)
                block = dense.at[at_x, at_z, core, span]
                slot = (step, 0, along, (-side) % 4)
                device = peer(0, side) if along else peer(side, 0)
                copy = remote(block, block, dense_send.at[slot], dense_recv.at[slot], device)
                copy.start()
                sent.append(copy)

    def dense_two(step, dense):
        for along in range(2):
            span = pl.ds(along * (CHUNK // 2), CHUNK // 2)
            for off in (3, 1, 2):
                if along:
                    block = dense.at[at_x, (at_z + off) % 4, core, span]
                else:
                    block = dense.at[(at_x + off) % 4, at_z, core, span]
                remote(
                    block, block, dense_send.at[step, 0, along, off], dense_recv.at[step, 0, along, off], sibling
                ).wait_recv()
        for along in range(2):
            span = pl.ds(along * (CHUNK // 2), CHUNK // 2)
            for side in SIDES:
                block = dense.at[at_x, :, core, span] if along else dense.at[:, at_z, core, span]
                device = peer(side, 0) if along else peer(0, side)
                slot = (step, 1, along, (-side) % 4)
                copy = remote(block, block, dense_send.at[slot], dense_recv.at[slot], device)
                copy.start()
                sent.append(copy)

    def dense_three(step, dense):
        for along in range(2):
            span = pl.ds(along * (CHUNK // 2), CHUNK // 2)
            for off in (3, 1, 2):
                block = (
                    dense.at[(at_x + off) % 4, :, core, span] if along else dense.at[:, (at_z + off) % 4, core, span]
                )
                remote(
                    block, block, dense_send.at[step, 1, along, off], dense_recv.at[step, 1, along, off], sibling
                ).wait_recv()
        block = dense.at[:, :, core]
        copy = remote(block, block, dense_send.at[step, 2, 0, 0], dense_recv.at[step, 2, 0, 0], sibling)
        copy.start()
        sent.append(copy)

    def dense_done(step, dense):
        block = dense.at[:, :, 1 - core]
        remote(block, block, dense_send.at[step, 2, 0, 0], dense_recv.at[step, 2, 0, 0], sibling).wait_recv()

    def image_start(step, image, scalars):
        image_out[step, pl.ds(0, ROW_BLOCKS), :] = image
        image_out[step, pl.ds(ROW_BLOCKS, 8), :] = scalar_rows(scalars)
        for side in SIDES:
            back = (-side) % 4
            copy = remote(
                image_out.at[step],
                image_in.at[step, back],
                image_send.at[step, back],
                image_recv.at[step, back],
                peer(0, 0, 0, side),
            )
            copy.start()
            sent.append(copy)

    def image_finish(step):
        for off in (3, 1, 2):
            block = image_in.at[step, off]
            remote(block, block, image_send.at[step, off], image_recv.at[step, off], sibling).wait_recv()
        parts = [image_out[step]] + [image_in[step, off] for off in (1, 2, 3)]
        total = tree4(parts)
        return total[:ROW_BLOCKS], total[ROW_BLOCKS:]

    def norm_sum(scalars):
        value = scalar_rows(scalars)
        for axis in range(2):
            norm_out[axis] = value
            for side in SIDES:
                back = (-side) % 4
                device = peer(0, side) if axis else peer(side, 0)
                copy = remote(
                    norm_out.at[axis], norm_in.at[axis, back], norm_send.at[axis, back], norm_recv.at[axis, back], device
                )
                copy.start()
                sent.append(copy)
            for off in (3, 1, 2):
                block = norm_in.at[axis, off]
                remote(block, block, norm_send.at[axis, off], norm_recv.at[axis, off], sibling).wait_recv()
            value = tree4([value] + [norm_in[axis, off] for off in (1, 2, 3)])
        norm_out[2] = value
        copy = remote(norm_out.at[2], norm_in.at[2, 0], norm_send.at[2, 0], norm_recv.at[2, 0], sibling)
        copy.start()
        sent.append(copy)
        copy.wait_recv()
        return value + norm_in[2, 0]

    def root(square):
        return jnp.sqrt(jnp.maximum(square, 0.0) + norm_eps)

    delays = delays_ref[...]
    pick_rows(delays)
    sums, scalars = back_and_gather(0, gather_first, [total_of(delays * delays)], True)
    beta_first = root(scalars[1:2])
    right_first = sums / beta_first
    right_slots, right_chunk = right_first[:SLOTS], right_first[SLOTS:]
    dense_one(0, dense_first, right_chunk)
    left_first = delays / beta_first

    image = forward(right_slots)
    image_start(0, image, [total_of(right_chunk * right_chunk)])
    dense_two(0, dense_first)
    image, scalars = image_finish(0)
    alpha_part = scalars[1:2, 0:1]

    pick_rows(image)
    scalars = [alpha_part, total_of(image * image), total_of(image * left_first), total_of(left_first * left_first)]
    dense_three(0, dense_first)
    sums, scalars = back_and_gather(1, gather_second, scalars, False)
    alpha_first = root(scalars[1:2])
    beta_second = root(
        scalars[2:3] / (alpha_first * alpha_first) - 2.0 * scalars[3:4] + alpha_first * alpha_first * scalars[4:5]
    )
    left_second = (image / alpha_first - alpha_first * left_first) / beta_second
    right_second = (sums / alpha_first - alpha_first * right_first) / beta_second
    right_second = right_second - beta_second * (right_first / alpha_first)
    right_slots, right_chunk = right_second[:SLOTS], right_second[SLOTS:]
    dense_one(1, dense_second, right_chunk)

    image = forward(right_slots)
    image_start(1, image, [total_of(right_chunk * right_chunk)])
    dense_two(1, dense_second)
    image, scalars = image_finish(1)
    alpha_part = scalars[1:2, 0:1]
    scalars = [alpha_part, total_of(image * image), total_of(image * left_second), total_of(left_second * left_second)]
    scalars = norm_sum(scalars)
    dense_three(1, dense_second)
    alpha_second = root(scalars[1:2])
    beta_third = root(
        scalars[2:3] / (alpha_second * alpha_second) - 2.0 * scalars[3:4] + alpha_second * alpha_second * scalars[4:5]
    )
    left_ref[...] = (image / alpha_second - alpha_second * left_second) / beta_third

    rho_first = jnp.sqrt(alpha_first * alpha_first + beta_second * beta_second)
    cosine = alpha_first / rho_first
    sine = beta_second / rho_first
    step_first = cosine * beta_first / rho_first
    phi_bar = sine * beta_first
    theta = sine * alpha_second
    rho_bar = -cosine * alpha_second
    rho_second = jnp.sqrt(rho_bar * rho_bar + beta_third * beta_third)
    step_second = rho_bar / rho_second * phi_bar / rho_second
    weight_first = (step_first - step_second * (theta / rho_first)) / alpha_first
    weight_second = step_second / alpha_second

    dense_done(0, dense_first)
    dense_done(1, dense_second)
    stores = []
    for off in range(4):
        for to_z in range(4):
            slow_buf[off, to_z] = dense_first[off, to_z] * weight_first + dense_second[off, to_z] * weight_second
        store = pltpu.make_async_copy(slow_buf.at[off], slow_hbm.at[off], store_sem.at[off])
        store.start()
        stores.append(store)
    for store in stores:
        store.wait()
    for copy in sent:
        copy.wait_send()


def shards(delays, kernel_tiles, row_blocks, col_blocks, tile_counts):
    dma = pltpu.SemaphoreType.DMA
    vmem = pl.BlockSpec(memory_space=pltpu.VMEM)
    dense_shape = (4, 4, 2, CHUNK, TILE)
    slowness, left = pl.pallas_call(
        lsqr_kernel,
        out_shape=(
            jax.ShapeDtypeStruct(dense_shape, F32),
            jax.ShapeDtypeStruct((ROW_BLOCKS, TILE), F32),
        ),
        in_specs=[
            pl.BlockSpec(memory_space=pltpu.SMEM),
            vmem,
            vmem,
            vmem,
            pl.BlockSpec(memory_space=pl.ANY),
        ],
        out_specs=(pl.BlockSpec(memory_space=pl.ANY), vmem),
        scratch_shapes=[
            pltpu.VMEM((SLOTS * TILE, TILE), BF16),
            pltpu.VMEM((SLOTS, 2 * TILE), F32),
            pltpu.VMEM((SLOTS, TILE), F32),
            pltpu.VMEM((2, 4, 4, BLOCK_ROWS, TILE), F32),
            pltpu.VMEM((2, 4, 4, BLOCK_ROWS, TILE), F32),
            pltpu.VMEM((2 * PAIR_ROWS, TILE), F32),
            pltpu.VMEM((SLOTS, TILE), BF16),
            pltpu.VMEM((ROW_BLOCKS, SLOTS), BF16),
            pltpu.VMEM((2 * PAIR_ROWS, 2 * TILE), F32),
            pltpu.VMEM((8, TILE), F32),
            pltpu.VMEM((8, TILE), F32),
            pltpu.VMEM((2, PAIR_ROWS + 8, TILE), F32),
            pltpu.VMEM((2, PAIR_ROWS + 8, TILE), F32),
            pltpu.VMEM((2, ROW_BLOCKS + 8, TILE), F32),
            pltpu.VMEM((2, 4, ROW_BLOCKS + 8, TILE), F32),
            pltpu.VMEM((3, 8, TILE), F32),
            pltpu.VMEM((3, 4, 8, TILE), F32),
            pltpu.VMEM(dense_shape, F32),
            pltpu.VMEM(dense_shape, F32),
            pltpu.VMEM(dense_shape, F32),
            dma((LOAD_CHUNKS,)),
            dma((4,)),
            dma((2, 2, 4, 4)),
            dma((2, 2, 4, 4)),
            dma((2,)),
            dma((2, 2)),
            dma((2, 4)),
            dma((2, 4)),
            dma((3, 4)),
            dma((3, 4)),
            dma((2, 3, 2, 4)),
            dma((2, 3, 2, 4)),
        ],
        compiler_params=pltpu.CompilerParams(
            collective_id=0, has_side_effects=True, vmem_limit_bytes=48 * 2**20
        ),
        cost_estimate=pl.CostEstimate(flops=2 * 10**9, bytes_accessed=12 * 2**20, transcendentals=0),
    )(
        tile_counts,
        delays.reshape(ROW_BLOCKS, TILE),
        row_blocks.reshape(2, HALF),
        col_blocks.reshape(2, HALF),
        kernel_tiles.reshape(SLOTS * TILE, TILE),
    )
    return slowness.reshape(-1), left.reshape(-1)


def solution(mesh):
    in_specs = (
        P("dp"),
        P("dp", "mp", None, None, None),
        P("dp", "mp", None),
        P("dp", "mp", None),
        P("dp", "mp"),
    )
    out_specs = (P("mp"), P("dp"))
    return jax.shard_map(shards, mesh=mesh, in_specs=in_specs, out_specs=out_specs, check_vma=False)
```

time: 386 us -> 92.7 us (0.24)
  blocking collectives: 229 us -> 0 us
  Pallas kernels: 0 us -> 87 us
  waiting for transfers between devices: 84.7 us -> 0 us
  matrix products: 27.8 us -> 0 us
  other arithmetic: 21.6 us -> 0 us
  between operations: 18.6 us -> 1.3 us
    psum x5 -> x0, blocking collectives: 229 us -> none  [the longest x3 200 us: beta_total(): return lax.psum(partial_sq, 'dp')]
    pallas_call x0 -> x1, Pallas kernels: none -> 87 us  [shards(): pl.pallas_call(lsqr_kernel, out_shape=(jax.ShapeDtypeStruct(dense_shape,...]
    psum x2 -> x0, waiting for transfers between devices: 84.7 us -> none  [model_combine(): total = lax.psum(back_partial, 'dp')]
    dot_general x6 -> x0, matrix products: 27.8 us -> none  [the longest x2 15.7 us: forward_block(): jnp.einsum('kij,kj->ki', tiles_blk, picked, preferred_element_type=jnp.fl...]
    reduce_sum x5 -> x0, other arithmetic: 6.56 us -> none  [the longest x2 3.88 us: shards(): data_partial_sq = jnp.sum(right_raw * right_raw)]
    scatter-add x2 -> x0, other arithmetic: 5.87 us -> none  [backward_block(): return jax.ops.segment_sum(products, cols_blk, num_segments=cell_count)]
    unnamed x10 -> x8, local copies, waits for them, and re-layouts: 0.03 us -> 4.18 us
    reshape x2 -> x0, other arithmetic: 4.02 us -> none  [shards(): return (slowness.reshape(-1), left_dir.reshape(-1))]
  transfers between devices with their start and end apart: 2 -> 0, of which waited for: 2 -> 0; matrix products, arithmetic and copies ran while one was open for 0% -> 0% of each run, Pallas kernels for 0% -> 0%
where the time goes in v1:
time: 92.7 us; the launch traced here: 92.5 us
  Pallas kernels  87 us (94%)
  local copies, waits for them, and re-layouts  4.18 us (5%)
  between operations  1.3 us (1%)
    pallas_call x1, Pallas kernels, shards(): pl.pallas_call(lsqr_kernel, out_shape=(jax.ShapeDtypeStruct(dense_shape,...  87 us
    unnamed x8, local copies, waits for them, and re-layouts  4.18 us

profile of v1, /device:TPU:1, one launch (start us, length us, event | category | flops | bytes accessed | tf_op | source)
XLA Modules:
  0.0 92.5 jit_solution(1127077458438063908)
XLA Ops:
  1.3 0.0 copy-start
  1.3 0.7 copy-done
  2.0 0.0 copy-start.1
  2.0 0.7 copy-done.1
  2.7 0.0 copy-start.2
  2.7 0.7 copy-done.2
  3.4 87.0 %shard_map.68 = (f32[4,4,2,128,128]{4,3,2,1,0:T(8,128)S(1)}, f32[64,128]{1,0:T(8,128)S(1)}) custom-call(s32[1,1]{1,0:T(1,128)S(6)} %copy.9.count_ref, f32[64,128]{1,0:T(8,128)S(1)} %bitcast.7, s32[2,128]{1,0:T(2,128)S(1)} %bitcast.9, s32[2,128]{1,0:T(2,128)S(1)} %bitcast.10, bf16[32768,128]{1,0:T(8,128)(2,1)} %bitcast.11), custom_call_target="tpu_custom_call" | custom-call | flops 2000000000 | bytes 12582912 | tf_op jit(solution)/shard_map/pallas_call | solution.py:475
  90.4 1.5 %copy.10 = f32[524288]{0:T(1024)} copy(f32[524288]{0:T(1024)S(1)} %bitcast.6) | data formatting | bytes 4194304
  91.9 0.6 copy.11
Async XLA Ops:
  1.3 0.8 copy-start
  2.0 0.7 copy-start.1
  2.7 0.7 copy-start.2

commit v2 on v1

--- a/solution.py
+++ b/solution.py
@@ -11,7 +11,7 @@
 ROW_BLOCKS = 64
 CELL_BLOCKS = 4096
 CHUNK = CELL_BLOCKS // 32
-PAIR_ROWS = SLOTS + CHUNK
+WANTED = SLOTS + CHUNK
 BLOCK_ROWS = HALF + 8
 GROUP = 8
 LOAD_CHUNKS = 8
@@ -45,25 +45,29 @@
 
 def lsqr_kernel(
     count_ref,
+    delays_hbm,
+    rows_hbm,
+    cols_hbm,
+    tiles_hbm,
+    slow_hbm,
+    left_ref,
     delays_ref,
     rows_ref,
     cols_ref,
-    tiles_hbm,
-    slow_hbm,
-    left_ref,
     tiles,
     picked,
     slot_products,
-    gather_first,
-    gather_second,
+    gathered,
     targets,
+    hits,
+    rhs,
     row_pick,
     row_sum,
-    summed,
-    cols_out,
-    cols_in,
-    pair_out,
-    pair_in,
+    cols_line,
+    sums_out,
+    sums_in,
+    chunk_out,
+    chunk_in,
     image_out,
     image_in,
     norm_out,
@@ -72,11 +76,16 @@
     dense_second,
     slow_buf,
     load_sem,
+    small_sem,
     store_sem,
     gather_send,
     gather_recv,
-    cols_sem,
-    pair_sem,
+    cols_send,
+    cols_recv,
+    sums_send,
+    sums_recv,
+    chunk_send,
+    chunk_recv,
     image_send,
     image_recv,
     norm_send,
@@ -99,6 +108,11 @@
             src_ref=src, dst_ref=dst, send_sem=send, recv_sem=recv, device_id=device, device_id_type=MESH
         )
 
+    smalls = []
+    for number, (src, dst) in enumerate(((delays_hbm, delays_ref), (rows_hbm, rows_ref), (cols_hbm, cols_ref))):
+        small = pltpu.make_async_copy(src, dst, small_sem.at[number])
+        small.start()
+        smalls.append(small)
     loads = []
     load_rows = SLOTS * TILE // LOAD_CHUNKS
     for part in range(LOAD_CHUNKS):
@@ -115,11 +129,22 @@
 
     sent = []
 
+    low_lanes = lax.broadcasted_iota(jnp.int32, (TILE, TILE), 1) < TILE // 2
+    lane_f = lax.broadcasted_iota(jnp.int32, (TILE, TILE), 1).astype(F32)
+    sub_i = lax.broadcasted_iota(jnp.int32, (TILE, TILE), 0)
+
+    def lane_swap(first, second):
+        low = low_lanes[: first.shape[0]]
+        return (
+            jnp.where(low, first, pltpu.roll(second, TILE // 2, 1)),
+            jnp.where(low, pltpu.roll(first, TILE // 2, 1), second),
+        )
+
+    for small in smalls:
+        small.wait()
     count = count_ref[0, 0]
     rows_f = rows_ref[...].astype(F32)
     cols_f = cols_ref[...].astype(F32)
-    lane_f = lax.broadcasted_iota(jnp.int32, (TILE, TILE), 1).astype(F32)
-    sub_i = lax.broadcasted_iota(jnp.int32, (TILE, TILE), 0)
     for half in range(2):
         down = jnp.transpose(jnp.broadcast_to(rows_f[half : half + 1, :], (TILE, TILE)))
         live = sub_i + half * HALF < count
@@ -128,15 +153,18 @@
         sub_r = lax.broadcasted_iota(jnp.int32, (ROW_BLOCKS, TILE), 0).astype(F32)
         lane_r = lax.broadcasted_iota(jnp.int32, (ROW_BLOCKS, TILE), 1) + half * HALF
         row_sum[:, pl.ds(half * HALF, HALF)] = jnp.where((across == sub_r) & (lane_r < count), 1.0, 0.0).astype(BF16)
-        targets[pl.ds(half * HALF, HALF), :] = jnp.transpose(
-            jnp.broadcast_to(cols_f[half : half + 1, :], (TILE, TILE))
-        )
-    first_block = ((dp // 2) * (2 * CHUNK)).astype(F32)
-    core_f = core.astype(F32)
-    chunk_f = sub_i.astype(F32) + first_block
-    targets[pl.ds(SLOTS, CHUNK), :] = chunk_f + core_f * CHUNK
-    targets[pl.ds(PAIR_ROWS + SLOTS, CHUNK), :] = chunk_f + (1.0 - core_f) * CHUNK
-    cols_out[...] = jnp.concatenate([cols_f, jnp.zeros((6, TILE), F32)], axis=0)
+    own_cols = jnp.concatenate([cols_f, jnp.zeros((6, TILE), F32)], axis=0)
+    for axis in range(2):
+        cols_line[axis, 0, 0] = own_cols
+
+    def target_rows(axis, off):
+        start = off * WANTED
+        for half in range(2):
+            targets[axis, pl.ds(start + half * HALF, HALF), :] = jnp.transpose(
+                jnp.broadcast_to(cols_line[1 - axis, 0, off, pl.ds(half, 1), :], (TILE, TILE))
+            )
+        device = peer(off, 0)[0] if axis else peer(0, off)[0]
+        targets[axis, pl.ds(start + SLOTS, CHUNK), :] = (sub_i + device * CHUNK).astype(F32)
 
     def pick_rows(vector):
         padded = jnp.concatenate([vector, jnp.zeros((TILE - ROW_BLOCKS, TILE), F32)], axis=0)
@@ -149,14 +177,14 @@
         span = pl.ds(group * GROUP, GROUP)
         return jnp.concatenate([picked[span, pl.ds(0, TILE)], picked[span, pl.ds(TILE, TILE)]], axis=0)
 
-    def back_group(group, block, first):
+    def back_group(group):
         parts = both_parts(group)
         lhs = jnp.concatenate(
             [jnp.where(row_in_group == slot, parts, 0.0).astype(BF16) for slot in range(GROUP)], axis=1
         )
         weights = tiles[pl.ds(group * (GROUP * TILE), GROUP * TILE), :]
         out = jnp.dot(lhs, weights, preferred_element_type=F32)
-        block[pl.ds((group - first) * GROUP, GROUP), :] = out[:GROUP] + out[GROUP:]
+        return out[:GROUP] + out[GROUP:]
 
     def forward_group(group):
         lhs = both_parts(group).astype(BF16)
@@ -168,134 +196,208 @@
             chosen = jnp.where(sub_group == slot, out[:, slot * TILE : (slot + 1) * TILE], chosen)
         slot_products[pl.ds(group * GROUP, GROUP), :] = chosen
 
-    def forward(right):
+    def forward(right, between):
         high, low = split_parts(right)
         picked[:, pl.ds(0, TILE)] = high.astype(F32)
         picked[:, pl.ds(TILE, TILE)] = low.astype(F32)
-
-        @pl.loop(0, SLOTS // GROUP, unroll=4)
+        half = SLOTS // GROUP // 2
+
+        @pl.loop(0, half, unroll=4)
         def _(group):
             forward_group(group)
 
+        result = between()
+
+        @pl.loop(half, 2 * half, unroll=4)
+        def _(group):
+            forward_group(group)
+
         out = jnp.dot(row_sum[...], side_by_side(slot_products[...]), preferred_element_type=F32)
-        return out[:, :TILE] + out[:, TILE:]
+        return out[:, :TILE] + out[:, TILE:], result
 
     def scalar_rows(scalars):
         rows = [jnp.broadcast_to(value, (1, TILE)) for value in scalars]
-        rows = [jnp.zeros((1, TILE), F32)] + rows
         rows += [jnp.zeros((8 - len(rows), TILE), F32)]
         return jnp.concatenate(rows, axis=0)
 
-    def back_and_gather(step, gathered, scalars, waits):
-        def arrival(half, off_x, off_z):
-            block = gathered.at[half, off_x, off_z]
-            return remote(
-                block, block, gather_send.at[step, half, off_x, off_z], gather_recv.at[step, half, off_x, off_z], sibling
+    def line(axis, off, core_off=0):
+        return peer(0, off, core_off) if axis else peer(off, 0, core_off)
+
+    def exchange_cols():
+        copies = []
+        for axis in range(2):
+            for side in SIDES:
+                back = (-side) % 4
+                copy = remote(
+                    cols_line.at[axis, 0, 0],
+                    cols_line.at[axis, 0, back],
+                    cols_send.at[axis, 0, back],
+                    cols_recv.at[axis, 0, back],
+                    line(axis, side),
+                )
+                copy.start()
+                copies.append(copy)
+        sent.extend(copies)
+        return copies
+
+    def spread_cols(copies):
+        for axis in range(2):
+            target_rows(axis, 0)
+        for copy in copies:
+            copy.wait_recv()
+        across = []
+        for axis in range(2):
+            copy = remote(
+                cols_line.at[axis, 0], cols_line.at[axis, 1], cols_send.at[axis, 1, 0], cols_recv.at[axis, 1, 0], sibling
             )
-
-        def send(half, off_x, off_z, side, along_x):
-            to_x, to_z = (off_x - side) % 4, (off_z - side) % 4
-            dst = (to_x, off_z) if along_x else (off_x, to_z)
-            device = peer(side, 0) if along_x else peer(0, side)
+            copy.start()
+            across.append(copy)
+        sent.extend(across)
+        for axis in range(2):
+            for off in (1, 2, 3):
+                target_rows(axis, off)
+        for copy in across:
+            copy.wait_recv()
+        for axis in range(2):
+
+            @pl.loop(0, 4 * WANTED // TILE)
+            def _(part):
+                span = pl.ds(part * TILE, TILE)
+                want = targets[axis, span, :]
+                for off in range(4):
+                    for core_off in range(2):
+                        for half in range(2):
+                            one = cols_line[axis, core_off, off, pl.ds(half, 1), :]
+                            column = ((off * 2 + core_off) * 2 + half) * HALF
+                            hits[axis, span, pl.ds(column, HALF)] = jnp.where(want == one, 1.0, 0.0).astype(BF16)
+
+    def back_and_gather(step, scalars, first_step):
+        def arrival(axis, core_off, off):
+            block = gathered.at[step, axis, core_off, off]
+            slot = (step, axis, core_off, off)
+            return remote(block, block, gather_send.at[slot], gather_recv.at[slot], sibling)
+
+        tail = scalar_rows(scalars)
+        for axis in range(2):
+            gathered[step, axis, 0, 0, pl.ds(HALF, 8), :] = tail
+        chunks = LOAD_CHUNKS // 2
+        groups = HALF // GROUP
+        per = groups // chunks
+        for part in range(chunks):
+            if first_step:
+                loads[part].wait()
+                loads[chunks + part].wait()
+
+            @pl.loop(0, per, unroll=per)
+            def _(index):
+                group = part * per + index
+                low, high = lane_swap(back_group(group), back_group(groups + group))
+                span = pl.ds(group * GROUP, GROUP)
+                gathered[step, 0, 0, 0, span, :] = low
+                gathered[step, 1, 0, 0, span, :] = high
+
+        if first_step:
+            pl.semaphore_wait(barrier, len(partners))
+            cols_copies = exchange_cols()
+
+        def send(axis, core_off, off, to_core, to_off, device):
+            slot = (step, axis, to_core, to_off)
             copy = remote(
-                gathered.at[half, off_x, off_z],
-                gathered.at[half, dst[0], dst[1]],
-                gather_send.at[step, half, dst[0], dst[1]],
-                gather_recv.at[step, half, dst[0], dst[1]],
+                gathered.at[step, axis, core_off, off],
+                gathered.at[slot],
+                gather_send.at[slot],
+                gather_recv.at[slot],
                 device,
             )
             copy.start()
             sent.append(copy)
 
-        chunks = LOAD_CHUNKS // 2
-        groups = HALF // GROUP
-        for half in range(2):
-            tail = scalar_rows(scalars)
-            lane_cols = jnp.broadcast_to(cols_f[half : half + 1, :], (8, TILE))
-            own = gathered.at[half, 0, 0]
-            own[pl.ds(HALF, 8), :] = jnp.where(sub_group == 0, lane_cols, tail)
-            for part in range(chunks):
-                if waits:
-                    loads[half * chunks + part].wait()
-                per = groups // chunks
-                start = half * groups + part * per
-
-                @pl.loop(0, per, unroll=per)
-                def _(index):
-                    back_group(start + index, own, half * groups)
-
-            if waits and half == 0:
-                pl.semaphore_wait(barrier, len(partners))
-                swap = remote(cols_out, cols_in, cols_sem.at[0], cols_sem.at[1], sibling)
-                swap.start()
-                sent.append(swap)
-            for side in SIDES:
-                send(half, 0, 0, side, half == 0)
-        for half in range(2):
-            for side in SIDES:
-                send(half, 0, 0, side, half == 1)
-        if waits:
-            swap.wait_recv()
-            other = cols_in[...]
-            for half in range(2):
-                targets[pl.ds(PAIR_ROWS + half * HALF, HALF), :] = jnp.transpose(
-                    jnp.broadcast_to(other[half : half + 1, :], (TILE, TILE))
-                )
+        for side in SIDES:
+            for axis in range(2):
+                send(axis, 0, 0, 0, (-side) % 4, line(axis, side))
+        for axis in range(2):
+            send(axis, 0, 0, 1, 0, sibling)
+        if first_step:
+            spread_cols(cols_copies)
         for off in (3, 1, 2):
-            arrival(0, off, 0).wait_recv()
-            for side in SIDES:
-                send(0, off, 0, side, False)
-            arrival(1, 0, off).wait_recv()
-            for side in SIDES:
-                send(1, 0, off, side, True)
-
-        order = [(0, 0)] + [(off, 0) for off in (3, 1, 2)] + [(0, off) for off in (3, 1, 2)]
-        order += [(off_x, off_z) for off_z in (3, 1, 2) for off_x in (3, 1, 2)]
-        for number, (off_x, off_z) in enumerate(order):
-            if off_z:
-                if off_x or not off_x:
-                    pass
-            if off_z != 0:
-                arrival(0, off_x, off_z).wait_recv()
-            if off_x != 0:
-                arrival(1, off_x, off_z).wait_recv()
-            values = jnp.concatenate(
-                [
-                    side_by_side(gathered[0, off_x, off_z, pl.ds(0, HALF), :]),
-                    side_by_side(gathered[1, off_x, off_z, pl.ds(0, HALF), :]),
-                ],
-                axis=0,
+            for axis in range(2):
+                arrival(axis, 0, off).wait_recv()
+                send(axis, 0, off, 1, off, sibling)
+
+        def take(axis, core_off, off):
+            block = gathered[step, axis, core_off, off, pl.ds(0, HALF), :]
+            high = block.astype(BF16).astype(F32)
+            first, second = lane_swap(high, block - high)
+            row = (off * 2 + core_off) * SLOTS
+            rhs[axis, pl.ds(row, HALF), :] = first.astype(BF16)
+            rhs[axis, pl.ds(row + HALF, HALF), :] = second.astype(BF16)
+
+        for axis in range(2):
+            for off in range(4):
+                take(axis, 0, off)
+        for axis in range(2):
+            for off in (0, 3, 1, 2):
+                arrival(axis, 1, off).wait_recv()
+                take(axis, 1, off)
+
+        line_scalars = tree4([gathered[step, 0, 0, off, pl.ds(HALF, 8), :] for off in range(4)])
+        line_scalars = line_scalars + tree4([gathered[step, 0, 1, off, pl.ds(HALF, 8), :] for off in range(4)])
+
+        def wanted_sums(axis, off, start, size):
+            out = jnp.dot(
+                hits[axis, pl.ds(off * WANTED + start, size), :], rhs[axis], preferred_element_type=F32
             )
-            ids = [gathered[half, off_x, off_z, pl.ds(HALF, 1), :] for half in range(2)]
-
-            @pl.loop(0, 2 * PAIR_ROWS // 256)
-            def _(part):
-                span = pl.ds(part * 256, 256)
-                want = targets[span, :]
-                hits = jnp.concatenate([jnp.where(want == one, 1.0, 0.0).astype(BF16) for one in ids], axis=1)
-                out = jnp.dot(hits, values, preferred_element_type=F32)
-                if number == 0:
-                    summed[span, :] = out
-                else:
-                    summed[span, :] = summed[span, :] + out
-
-        scalar_tree = tree4(
-            [tree4([gathered[0, off_x, off_z, pl.ds(HALF, 8), :] for off_x in range(4)]) for off_z in range(4)]
-        )
-        other_half = summed[pl.ds(PAIR_ROWS, PAIR_ROWS), :]
-        pair_out[step, pl.ds(0, PAIR_ROWS), :] = other_half[:, :TILE] + other_half[:, TILE:]
-        pair_out[step, pl.ds(PAIR_ROWS, 8), :] = scalar_tree
-        swap_sums = remote(
-            pair_out.at[step], pair_in.at[step], pair_sem.at[step, 0], pair_sem.at[step, 1], sibling
-        )
-        swap_sums.start()
-        sent.append(swap_sums)
-        mine = summed[pl.ds(0, PAIR_ROWS), :]
-        mine = mine[:, :TILE] + mine[:, TILE:]
-        swap_sums.wait_recv()
-        mine = mine + pair_in[step, pl.ds(0, PAIR_ROWS), :]
-        sums = scalar_tree + pair_in[step, pl.ds(PAIR_ROWS, 8), :]
-        return mine, sums
+            out = out + pltpu.roll(out, TILE // 2, 1)
+            return jnp.where(low_lanes[: size // 2], out[: size // 2], out[size // 2 :])
+
+        for axis in range(2):
+            for off in SIDES + (0,):
+                sums_out[step, axis, off, pl.ds(0, HALF), :] = wanted_sums(axis, off, 0, SLOTS)
+                sums_out[step, axis, off, pl.ds(HALF, 8), :] = line_scalars
+                if off:
+                    slot = (step, axis, (-off) % 4)
+                    copy = remote(
+                        sums_out.at[step, axis, off],
+                        sums_in.at[slot],
+                        sums_send.at[slot],
+                        sums_recv.at[slot],
+                        line(1 - axis, off),
+                    )
+                    copy.start()
+                    sent.append(copy)
+        for axis in range(2):
+            for off in SIDES + (0,):
+                chunk_out[step, axis, off] = wanted_sums(axis, off, SLOTS, CHUNK)
+                if off:
+                    slot = (step, axis, (-off) % 4)
+                    copy = remote(
+                        chunk_out.at[step, axis, off],
+                        chunk_in.at[slot],
+                        chunk_send.at[slot],
+                        chunk_recv.at[slot],
+                        line(1 - axis, off),
+                    )
+                    copy.start()
+                    sent.append(copy)
+        totals = []
+        for axis in range(2):
+            for off in (3, 1, 2):
+                block = sums_in.at[step, axis, off]
+                slot = (step, axis, off)
+                remote(block, block, sums_send.at[slot], sums_recv.at[slot], sibling).wait_recv()
+            totals.append(tree4([sums_out[step, axis, 0]] + [sums_in[step, axis, off] for off in (1, 2, 3)]))
+        mine = jnp.concatenate(lane_swap(totals[0][:HALF], totals[1][:HALF]), axis=0)
+        return mine, totals[0][HALF:]
+
+    def chunk_sums(step):
+        totals = []
+        for axis in range(2):
+            for off in (3, 1, 2):
+                block = chunk_in.at[step, axis, off]
+                slot = (step, axis, off)
+                remote(block, block, chunk_send.at[slot], chunk_recv.at[slot], sibling).wait_recv()
+            totals.append(tree4([chunk_out[step, axis, 0]] + [chunk_in[step, axis, off] for off in (1, 2, 3)]))
+        return jnp.concatenate(lane_swap(totals[0], totals[1]), axis=0)
 
     def dense_one(step, dense, chunk):
         dense[at_x, at_z, core] = chunk
@@ -400,44 +502,52 @@
 
     delays = delays_ref[...]
     pick_rows(delays)
-    sums, scalars = back_and_gather(0, gather_first, [total_of(delays * delays)], True)
-    beta_first = root(scalars[1:2])
+    sums, scalars = back_and_gather(0, [total_of(delays * delays)], True)
+    beta_first = root(scalars[0:1])
     right_first = sums / beta_first
-    right_slots, right_chunk = right_first[:SLOTS], right_first[SLOTS:]
-    dense_one(0, dense_first, right_chunk)
     left_first = delays / beta_first
 
-    image = forward(right_slots)
-    image_start(0, image, [total_of(right_chunk * right_chunk)])
+    def finish_first():
+        chunk = chunk_sums(0) / beta_first
+        dense_one(0, dense_first, chunk)
+        return chunk
+
+    image, chunk_first = forward(right_first, finish_first)
+    image_start(0, image, [total_of(chunk_first * chunk_first)])
     dense_two(0, dense_first)
     image, scalars = image_finish(0)
-    alpha_part = scalars[1:2, 0:1]
+    alpha_part = scalars[0:1, 0:1]
 
     pick_rows(image)
     scalars = [alpha_part, total_of(image * image), total_of(image * left_first), total_of(left_first * left_first)]
     dense_three(0, dense_first)
-    sums, scalars = back_and_gather(1, gather_second, scalars, False)
-    alpha_first = root(scalars[1:2])
+    sums, scalars = back_and_gather(1, scalars, False)
+    alpha_first = root(scalars[0:1])
     beta_second = root(
-        scalars[2:3] / (alpha_first * alpha_first) - 2.0 * scalars[3:4] + alpha_first * alpha_first * scalars[4:5]
+        scalars[1:2] / (alpha_first * alpha_first) - 2.0 * scalars[2:3] + alpha_first * alpha_first * scalars[3:4]
     )
     left_second = (image / alpha_first - alpha_first * left_first) / beta_second
-    right_second = (sums / alpha_first - alpha_first * right_first) / beta_second
-    right_second = right_second - beta_second * (right_first / alpha_first)
-    right_slots, right_chunk = right_second[:SLOTS], right_second[SLOTS:]
-    dense_one(1, dense_second, right_chunk)
-
-    image = forward(right_slots)
-    image_start(1, image, [total_of(right_chunk * right_chunk)])
+
+    def second_right(back, right):
+        fresh = (back / alpha_first - alpha_first * right) / beta_second
+        return fresh - beta_second * (right / alpha_first)
+
+    def finish_second():
+        chunk = second_right(chunk_sums(1), chunk_first)
+        dense_one(1, dense_second, chunk)
+        return chunk
+
+    image, chunk_second = forward(second_right(sums, right_first), finish_second)
+    image_start(1, image, [total_of(chunk_second * chunk_second)])
     dense_two(1, dense_second)
     image, scalars = image_finish(1)
-    alpha_part = scalars[1:2, 0:1]
+    alpha_part = scalars[0:1, 0:1]
     scalars = [alpha_part, total_of(image * image), total_of(image * left_second), total_of(left_second * left_second)]
     scalars = norm_sum(scalars)
     dense_three(1, dense_second)
-    alpha_second = root(scalars[1:2])
+    alpha_second = root(scalars[0:1])
     beta_third = root(
-        scalars[2:3] / (alpha_second * alpha_second) - 2.0 * scalars[3:4] + alpha_second * alpha_second * scalars[4:5]
+        scalars[1:2] / (alpha_second * alpha_second) - 2.0 * scalars[2:3] + alpha_second * alpha_second * scalars[3:4]
     )
     left_ref[...] = (image / alpha_second - alpha_second * left_second) / beta_third
 
@@ -471,6 +581,7 @@
 def shards(delays, kernel_tiles, row_blocks, col_blocks, tile_counts):
     dma = pltpu.SemaphoreType.DMA
     vmem = pl.BlockSpec(memory_space=pltpu.VMEM)
+    hbm = pl.BlockSpec(memory_space=pl.ANY)
     dense_shape = (4, 4, 2, CHUNK, TILE)
     slowness, left = pl.pallas_call(
         lsqr_kernel,
@@ -478,28 +589,26 @@
             jax.ShapeDtypeStruct(dense_shape, F32),
             jax.ShapeDtypeStruct((ROW_BLOCKS, TILE), F32),
         ),
-        in_specs=[
-            pl.BlockSpec(memory_space=pltpu.SMEM),
-            vmem,
-            vmem,
-            vmem,
-            pl.BlockSpec(memory_space=pl.ANY),
-        ],
-        out_specs=(pl.BlockSpec(memory_space=pl.ANY), vmem),
+        in_specs=[pl.BlockSpec(memory_space=pltpu.SMEM)] + [hbm] * 4,
+        out_specs=(hbm, vmem),
         scratch_shapes=[
+            pltpu.VMEM((ROW_BLOCKS, TILE), F32),
+            pltpu.VMEM((2, HALF), jnp.int32),
+            pltpu.VMEM((2, HALF), jnp.int32),
             pltpu.VMEM((SLOTS * TILE, TILE), BF16),
             pltpu.VMEM((SLOTS, 2 * TILE), F32),
             pltpu.VMEM((SLOTS, TILE), F32),
-            pltpu.VMEM((2, 4, 4, BLOCK_ROWS, TILE), F32),
-            pltpu.VMEM((2, 4, 4, BLOCK_ROWS, TILE), F32),
-            pltpu.VMEM((2 * PAIR_ROWS, TILE), F32),
+            pltpu.VMEM((2, 2, 2, 4, BLOCK_ROWS, TILE), F32),
+            pltpu.VMEM((2, 4 * WANTED, TILE), F32),
+            pltpu.VMEM((2, 4 * WANTED, 8 * SLOTS), BF16),
+            pltpu.VMEM((2, 8 * SLOTS, TILE), BF16),
             pltpu.VMEM((SLOTS, TILE), BF16),
             pltpu.VMEM((ROW_BLOCKS, SLOTS), BF16),
-            pltpu.VMEM((2 * PAIR_ROWS, 2 * TILE), F32),
-            pltpu.VMEM((8, TILE), F32),
-            pltpu.VMEM((8, TILE), F32),
-            pltpu.VMEM((2, PAIR_ROWS + 8, TILE), F32),
-            pltpu.VMEM((2, PAIR_ROWS + 8, TILE), F32),
+            pltpu.VMEM((2, 2, 4, 8, TILE), F32),
+            pltpu.VMEM((2, 2, 4, BLOCK_ROWS, TILE), F32),
+            pltpu.VMEM((2, 2, 4, BLOCK_ROWS, TILE), F32),
+            pltpu.VMEM((2, 2, 4, CHUNK // 2, TILE), F32),
+            pltpu.VMEM((2, 2, 4, CHUNK // 2, TILE), F32),
             pltpu.VMEM((2, ROW_BLOCKS + 8, TILE), F32),
             pltpu.VMEM((2, 4, ROW_BLOCKS + 8, TILE), F32),
             pltpu.VMEM((3, 8, TILE), F32),
@@ -508,11 +617,16 @@
             pltpu.VMEM(dense_shape, F32),
             pltpu.VMEM(dense_shape, F32),
             dma((LOAD_CHUNKS,)),
+            dma((3,)),
             dma((4,)),
-            dma((2, 2, 4, 4)),
-            dma((2, 2, 4, 4)),
-            dma((2,)),
-            dma((2, 2)),
+            dma((2, 2, 2, 4)),
+            dma((2, 2, 2, 4)),
+            dma((2, 2, 4)),
+            dma((2, 2, 4)),
+            dma((2, 2, 4)),
+            dma((2, 2, 4)),
+            dma((2, 2, 4)),
+            dma((2, 2, 4)),
             dma((2, 4)),
             dma((2, 4)),
             dma((3, 4)),

time: 92.7 us -> 83.2 us (0.90)
  Pallas kernels: 87 us -> 77.5 us
    pallas_call x1, Pallas kernels: 87 us -> 77.5 us  [shards(): pl.pallas_call(lsqr_kernel, out_shape=(jax.ShapeDtypeStruct(dense_shape,...]
where the time goes in v2:
time: 83.2 us; the launch traced here: 83 us
  Pallas kernels  77.5 us (93%)
  local copies, waits for them, and re-layouts  4.18 us (5%)
  between operations  1.3 us (2%)
    pallas_call x1, Pallas kernels, shards(): pl.pallas_call(lsqr_kernel, out_shape=(jax.ShapeDtypeStruct(dense_shape,...  77.5 us
    unnamed x8, local copies, waits for them, and re-layouts  4.18 us

profile of v2, /device:TPU:1, one launch (start us, length us, event | category | flops | bytes accessed | tf_op | source)
XLA Modules:
  0.0 83.0 jit_solution(14212453735760714571)
XLA Ops:
  1.3 0.0 copy-start
  1.3 0.7 copy-done
  2.0 0.0 copy-start.1
  2.0 0.7 copy-done.1
  2.7 0.0 copy-start.2
  2.7 0.7 copy-done.2
  3.4 77.5 %shard_map.68 = (f32[4,4,2,128,128]{4,3,2,1,0:T(8,128)S(1)}, f32[64,128]{1,0:T(8,128)S(1)}) custom-call(s32[1,1]{1,0:T(1,128)S(6)} %copy.9.count_ref, f32[64,128]{1,0:T(8,128)S(1)} %bitcast.7, s32[2,128]{1,0:T(2,128)S(1)} %bitcast.9, s32[2,128]{1,0:T(2,128)S(1)} %bitcast.10, bf16[32768,128]{1,0:T(8,128)(2,1)} %bitcast.11), custom_call_target="tpu_custom_call" | custom-call | flops 2000000000 | bytes 12582912 | tf_op jit(solution)/shard_map/pallas_call | solution.py:586
  80.9 1.5 %copy.10 = f32[524288]{0:T(1024)} copy(f32[524288]{0:T(1024)S(1)} %bitcast.6) | data formatting | bytes 4194304
  82.3 0.6 copy.11
Async XLA Ops:
  1.3 0.8 copy-start
  2.0 0.7 copy-start.1
  2.7 0.7 copy-start.2

commit v3 on v2

--- a/solution.py
+++ b/solution.py
@@ -11,7 +11,6 @@
 ROW_BLOCKS = 64
 CELL_BLOCKS = 4096
 CHUNK = CELL_BLOCKS // 32
-WANTED = SLOTS + CHUNK
 BLOCK_ROWS = HALF + 8
 GROUP = 8
 LOAD_CHUNKS = 8
@@ -22,7 +21,7 @@
 BF16 = jnp.bfloat16
 NT = (((1,), (1,)), ((), ()))
 
-SIDES = (1, 3, 2)
+SIDES = (2, 1, 3)
 
 
 def split_parts(values):
@@ -59,7 +58,8 @@
     slot_products,
     gathered,
     targets,
-    hits,
+    slot_hits,
+    chunk_hits,
     rhs,
     row_pick,
     row_sum,
@@ -113,13 +113,13 @@
         small = pltpu.make_async_copy(src, dst, small_sem.at[number])
         small.start()
         smalls.append(small)
-    loads = []
     load_rows = SLOTS * TILE // LOAD_CHUNKS
-    for part in range(LOAD_CHUNKS):
+    loads = [None] * LOAD_CHUNKS
+    for part in [p for q in range(LOAD_CHUNKS // 2) for p in (q, q + LOAD_CHUNKS // 2)]:
         span = pl.ds(part * load_rows, load_rows)
         load = pltpu.make_async_copy(tiles_hbm.at[span], tiles.at[span], load_sem.at[part])
         load.start()
-        loads.append(load)
+        loads[part] = load
 
     barrier = pltpu.get_barrier_semaphore()
     partners = [peer(side, 0) for side in SIDES] + [peer(0, side) for side in SIDES]
@@ -157,14 +157,11 @@
     for axis in range(2):
         cols_line[axis, 0, 0] = own_cols
 
-    def target_rows(axis, off):
-        start = off * WANTED
-        for half in range(2):
-            targets[axis, pl.ds(start + half * HALF, HALF), :] = jnp.transpose(
-                jnp.broadcast_to(cols_line[1 - axis, 0, off, pl.ds(half, 1), :], (TILE, TILE))
-            )
-        device = peer(off, 0)[0] if axis else peer(0, off)[0]
-        targets[axis, pl.ds(start + SLOTS, CHUNK), :] = (sub_i + device * CHUNK).astype(F32)
+    def slot_targets(axis):
+        wanted = jnp.concatenate([cols_line[1 - axis, 0, off, pl.ds(0, 2), :] for off in range(4)], axis=0)
+        down = jnp.transpose(jnp.concatenate([wanted, jnp.zeros((TILE - 8, TILE), F32)], axis=0))
+        for part in range(8):
+            targets[axis, pl.ds(part * HALF, HALF), :] = jnp.broadcast_to(down[:, part : part + 1], (HALF, TILE))
 
     def pick_rows(vector):
         padded = jnp.concatenate([vector, jnp.zeros((TILE - ROW_BLOCKS, TILE), F32)], axis=0)
@@ -202,13 +199,13 @@
         picked[:, pl.ds(TILE, TILE)] = low.astype(F32)
         half = SLOTS // GROUP // 2
 
-        @pl.loop(0, half, unroll=4)
+        @pl.loop(0, half, unroll=8)
         def _(group):
             forward_group(group)
 
         result = between()
 
-        @pl.loop(half, 2 * half, unroll=4)
+        @pl.loop(half, 2 * half, unroll=8)
         def _(group):
             forward_group(group)
 
@@ -240,9 +237,32 @@
         sent.extend(copies)
         return copies
 
+    def mark(dst, axis, span, want, core_off):
+        for off in range(4):
+            for half in range(2):
+                one = cols_line[axis, core_off, off, pl.ds(half, 1), :]
+                column = ((core_off * 4 + off) * 2 + half) * HALF
+                dst[axis, span, pl.ds(column, HALF)] = jnp.where(want == one, 1.0, 0.0).astype(BF16)
+
+    def mark_slots(core_off):
+        for axis in range(2):
+
+            @pl.loop(0, 4 * SLOTS // TILE)
+            def _(part):
+                span = pl.ds(part * TILE, TILE)
+                mark(slot_hits, axis, span, targets[axis, span, :], core_off)
+
+    def mark_chunks():
+        for axis in range(2):
+
+            @pl.loop(0, 4)
+            def _(off):
+                device = peer(off, 0)[0] if axis else peer(0, off)[0]
+                want = (sub_i + device * CHUNK).astype(F32)
+                for core_off in range(2):
+                    mark(chunk_hits, axis, pl.ds(off * CHUNK, CHUNK), want, core_off)
+
     def spread_cols(copies):
-        for axis in range(2):
-            target_rows(axis, 0)
         for copy in copies:
             copy.wait_recv()
         across = []
@@ -254,27 +274,17 @@
             across.append(copy)
         sent.extend(across)
         for axis in range(2):
-            for off in (1, 2, 3):
-                target_rows(axis, off)
+            slot_targets(axis)
+        mark_slots(0)
         for copy in across:
             copy.wait_recv()
-        for axis in range(2):
-
-            @pl.loop(0, 4 * WANTED // TILE)
-            def _(part):
-                span = pl.ds(part * TILE, TILE)
-                want = targets[axis, span, :]
-                for off in range(4):
-                    for core_off in range(2):
-                        for half in range(2):
-                            one = cols_line[axis, core_off, off, pl.ds(half, 1), :]
-                            column = ((off * 2 + core_off) * 2 + half) * HALF
-                            hits[axis, span, pl.ds(column, HALF)] = jnp.where(want == one, 1.0, 0.0).astype(BF16)
+        mark_slots(1)
 
     def back_and_gather(step, scalars, first_step):
-        def arrival(axis, core_off, off):
-            block = gathered.at[step, axis, core_off, off]
-            slot = (step, axis, core_off, off)
+        def arrival(axis, off, piece):
+            span = (pl.ds(0, HALF // 2), pl.ds(HALF // 2, BLOCK_ROWS - HALF // 2))[piece]
+            block = gathered.at[step, axis, 0, off, span]
+            slot = (piece, step, axis, 0, off)
             return remote(block, block, gather_send.at[slot], gather_recv.at[slot], sibling)
 
         tail = scalar_rows(scalars)
@@ -283,6 +293,25 @@
         chunks = LOAD_CHUNKS // 2
         groups = HALF // GROUP
         per = groups // chunks
+        def send(axis, to_off, device, piece):
+            span = (pl.ds(0, HALF // 2), pl.ds(HALF // 2, BLOCK_ROWS - HALF // 2))[piece]
+            copy = remote(
+                gathered.at[step, axis, 0, 0, span],
+                gathered.at[step, axis, 0, to_off, span],
+                gather_send.at[piece, step, axis, 0, to_off],
+                gather_recv.at[piece, step, axis, 0, to_off],
+                device,
+            )
+            copy.start()
+            sent.append(copy)
+
+        def across(axis, off):
+            block = gathered.at[step, axis, 0, off]
+            slot = (0, step, axis, 1, off)
+            copy = remote(block, gathered.at[step, axis, 1, off], gather_send.at[slot], gather_recv.at[slot], sibling)
+            copy.start()
+            sent.append(copy)
+
         for part in range(chunks):
             if first_step:
                 loads[part].wait()
@@ -296,39 +325,29 @@
                 gathered[step, 0, 0, 0, span, :] = low
                 gathered[step, 1, 0, 0, span, :] = high
 
-        if first_step:
-            pl.semaphore_wait(barrier, len(partners))
-            cols_copies = exchange_cols()
-
-        def send(axis, core_off, off, to_core, to_off, device):
-            slot = (step, axis, to_core, to_off)
-            copy = remote(
-                gathered.at[step, axis, core_off, off],
-                gathered.at[slot],
-                gather_send.at[slot],
-                gather_recv.at[slot],
-                device,
-            )
-            copy.start()
-            sent.append(copy)
-
-        for side in SIDES:
-            for axis in range(2):
-                send(axis, 0, 0, 0, (-side) % 4, line(axis, side))
-        for axis in range(2):
-            send(axis, 0, 0, 1, 0, sibling)
+            if 2 * (part + 1) % chunks == 0:
+                piece = 2 * (part + 1) // chunks - 1
+                if first_step and piece == 0:
+                    pl.semaphore_wait(barrier, len(partners))
+                    cols_copies = exchange_cols()
+                for side in SIDES:
+                    for axis in range(2):
+                        send(axis, (-side) % 4, line(axis, side), piece)
+        for axis in range(2):
+            across(axis, 0)
         if first_step:
             spread_cols(cols_copies)
         for off in (3, 1, 2):
             for axis in range(2):
-                arrival(axis, 0, off).wait_recv()
-                send(axis, 0, off, 1, off, sibling)
+                for piece in range(2):
+                    arrival(axis, off, piece).wait_recv()
+                across(axis, off)
 
         def take(axis, core_off, off):
             block = gathered[step, axis, core_off, off, pl.ds(0, HALF), :]
             high = block.astype(BF16).astype(F32)
             first, second = lane_swap(high, block - high)
-            row = (off * 2 + core_off) * SLOTS
+            row = (core_off * 4 + off) * SLOTS
             rhs[axis, pl.ds(row, HALF), :] = first.astype(BF16)
             rhs[axis, pl.ds(row + HALF, HALF), :] = second.astype(BF16)
 
@@ -337,22 +356,22 @@
                 take(axis, 0, off)
         for axis in range(2):
             for off in (0, 3, 1, 2):
-                arrival(axis, 1, off).wait_recv()
+                block = gathered.at[step, axis, 1, off]
+                slot = (0, step, axis, 1, off)
+                remote(block, block, gather_send.at[slot], gather_recv.at[slot], sibling).wait_recv()
                 take(axis, 1, off)
 
         line_scalars = tree4([gathered[step, 0, 0, off, pl.ds(HALF, 8), :] for off in range(4)])
         line_scalars = line_scalars + tree4([gathered[step, 0, 1, off, pl.ds(HALF, 8), :] for off in range(4)])
 
-        def wanted_sums(axis, off, start, size):
-            out = jnp.dot(
-                hits[axis, pl.ds(off * WANTED + start, size), :], rhs[axis], preferred_element_type=F32
-            )
+        def wanted_sums(hits, axis, off, size):
+            out = jnp.dot(hits[axis, pl.ds(off * size, size), :], rhs[axis], preferred_element_type=F32)
             out = out + pltpu.roll(out, TILE // 2, 1)
             return jnp.where(low_lanes[: size // 2], out[: size // 2], out[size // 2 :])
 
         for axis in range(2):
             for off in SIDES + (0,):
-                sums_out[step, axis, off, pl.ds(0, HALF), :] = wanted_sums(axis, off, 0, SLOTS)
+                sums_out[step, axis, off, pl.ds(0, HALF), :] = wanted_sums(slot_hits, axis, off, SLOTS)
                 sums_out[step, axis, off, pl.ds(HALF, 8), :] = line_scalars
                 if off:
                     slot = (step, axis, (-off) % 4)
@@ -365,9 +384,11 @@
                     )
                     copy.start()
                     sent.append(copy)
+        if first_step:
+            mark_chunks()
         for axis in range(2):
             for off in SIDES + (0,):
-                chunk_out[step, axis, off] = wanted_sums(axis, off, SLOTS, CHUNK)
+                chunk_out[step, axis, off] = wanted_sums(chunk_hits, axis, off, CHUNK)
                 if off:
                     slot = (step, axis, (-off) % 4)
                     copy = remote(
@@ -379,6 +400,8 @@
                     )
                     copy.start()
                     sent.append(copy)
+        if not first_step:
+            dense_three(0, dense_first, (0, 3, 1, 2))
         totals = []
         for axis in range(2):
             for off in (3, 1, 2):
@@ -432,24 +455,35 @@
                 copy.start()
                 sent.append(copy)
 
-    def dense_three(step, dense):
-        for along in range(2):
-            span = pl.ds(along * (CHUNK // 2), CHUNK // 2)
-            for off in (3, 1, 2):
-                block = (
-                    dense.at[(at_x + off) % 4, :, core, span] if along else dense.at[:, (at_z + off) % 4, core, span]
-                )
-                remote(
-                    block, block, dense_send.at[step, 1, along, off], dense_recv.at[step, 1, along, off], sibling
-                ).wait_recv()
-        block = dense.at[:, :, core]
-        copy = remote(block, block, dense_send.at[step, 2, 0, 0], dense_recv.at[step, 2, 0, 0], sibling)
-        copy.start()
-        sent.append(copy)
+    def dense_three(step, dense, offs):
+        for off in offs:
+            for along in range(2):
+                span = pl.ds(along * (CHUNK // 2), CHUNK // 2)
+                if off == 0:
+                    slot = (step, 2, along, 0)
+                    block = dense.at[at_x, :, core, span] if along else dense.at[:, at_z, core, span]
+                else:
+                    slot = (step, 1, along, off)
+                    if along:
+                        block = dense.at[(at_x + off) % 4, :, core, span]
+                    else:
+                        block = dense.at[:, (at_z + off) % 4, core, span]
+                    remote(block, block, dense_send.at[slot], dense_recv.at[slot], sibling).wait_recv()
+                    slot = (step, 2, along, off)
+                copy = remote(block, block, dense_send.at[slot], dense_recv.at[slot], sibling)
+                copy.start()
+                sent.append(copy)
 
     def dense_done(step, dense):
-        block = dense.at[:, :, 1 - core]
-        remote(block, block, dense_send.at[step, 2, 0, 0], dense_recv.at[step, 2, 0, 0], sibling).wait_recv()
+        for off in range(4):
+            for along in range(2):
+                span = pl.ds(along * (CHUNK // 2), CHUNK // 2)
+                if along:
+                    block = dense.at[(at_x + off) % 4, :, 1 - core, span]
+                else:
+                    block = dense.at[:, (at_z + off) % 4, 1 - core, span]
+                slot = (step, 2, along, off)
+                remote(block, block, dense_send.at[slot], dense_recv.at[slot], sibling).wait_recv()
 
     def image_start(step, image, scalars):
         image_out[step, pl.ds(0, ROW_BLOCKS), :] = image
@@ -474,28 +508,25 @@
         total = tree4(parts)
         return total[:ROW_BLOCKS], total[ROW_BLOCKS:]
 
-    def norm_sum(scalars):
+    def norm_sum(scalars, between):
         value = scalar_rows(scalars)
-        for axis in range(2):
-            norm_out[axis] = value
-            for side in SIDES:
-                back = (-side) % 4
-                device = peer(0, side) if axis else peer(side, 0)
-                copy = remote(
-                    norm_out.at[axis], norm_in.at[axis, back], norm_send.at[axis, back], norm_recv.at[axis, back], device
-                )
-                copy.start()
-                sent.append(copy)
-            for off in (3, 1, 2):
-                block = norm_in.at[axis, off]
-                remote(block, block, norm_send.at[axis, off], norm_recv.at[axis, off], sibling).wait_recv()
-            value = tree4([value] + [norm_in[axis, off] for off in (1, 2, 3)])
-        norm_out[2] = value
-        copy = remote(norm_out.at[2], norm_in.at[2, 0], norm_send.at[2, 0], norm_recv.at[2, 0], sibling)
-        copy.start()
-        sent.append(copy)
-        copy.wait_recv()
-        return value + norm_in[2, 0]
+        norm_out[...] = value
+        offs = [(x, z, c) for x in (2, 1, 3, 0) for z in (2, 1, 3, 0) for c in (1, 0) if (x, z, c) != (0, 0, 0)]
+        for x, z, c in offs:
+            slot = ((-x) % 4, (-z) % 4, c)
+            copy = remote(norm_out, norm_in.at[slot], norm_send.at[slot], norm_recv.at[slot], peer(x, z, c))
+            copy.start()
+            sent.append(copy)
+        between()
+        for slot in offs:
+            block = norm_in.at[slot]
+            remote(block, block, norm_send.at[slot], norm_recv.at[slot], sibling).wait_recv()
+        parts = {slot: norm_in[slot] for slot in offs}
+        parts[0, 0, 0] = value
+        lines = [
+            tree4([tree4([parts[x, z, c] for x in range(4)]) for z in range(4)]) for c in range(2)
+        ]
+        return lines[0] + lines[1]
 
     def root(square):
         return jnp.sqrt(jnp.maximum(square, 0.0) + norm_eps)
@@ -520,7 +551,6 @@
 
     pick_rows(image)
     scalars = [alpha_part, total_of(image * image), total_of(image * left_first), total_of(left_first * left_first)]
-    dense_three(0, dense_first)
     sums, scalars = back_and_gather(1, scalars, False)
     alpha_first = root(scalars[0:1])
     beta_second = root(
@@ -543,8 +573,7 @@
     image, scalars = image_finish(1)
     alpha_part = scalars[0:1, 0:1]
     scalars = [alpha_part, total_of(image * image), total_of(image * left_second), total_of(left_second * left_second)]
-    scalars = norm_sum(scalars)
-    dense_three(1, dense_second)
+    scalars = norm_sum(scalars, lambda: dense_three(1, dense_second, (0, 3, 1, 2)))
     alpha_second = root(scalars[0:1])
     beta_third = root(
         scalars[1:2] / (alpha_second * alpha_second) - 2.0 * scalars[2:3] + alpha_second * alpha_second * scalars[3:4]
@@ -581,7 +610,8 @@
 def shards(delays, kernel_tiles, row_blocks, col_blocks, tile_counts):
     dma = pltpu.SemaphoreType.DMA
     vmem = pl.BlockSpec(memory_space=pltpu.VMEM)
-    hbm = pl.BlockSpec(memory_space=pl.ANY)
+    hbm = pl.BlockSpec(memory_space=pltpu.HBM)
+    anywhere = pl.BlockSpec(memory_space=pl.ANY)
     dense_shape = (4, 4, 2, CHUNK, TILE)
     slowness, left = pl.pallas_call(
         lsqr_kernel,
@@ -590,7 +620,7 @@
             jax.ShapeDtypeStruct((ROW_BLOCKS, TILE), F32),
         ),
         in_specs=[pl.BlockSpec(memory_space=pltpu.SMEM)] + [hbm] * 4,
-        out_specs=(hbm, vmem),
+        out_specs=(anywhere, vmem),
         scratch_shapes=[
             pltpu.VMEM((ROW_BLOCKS, TILE), F32),
             pltpu.VMEM((2, HALF), jnp.int32),
@@ -599,8 +629,9 @@
             pltpu.VMEM((SLOTS, 2 * TILE), F32),
             pltpu.VMEM((SLOTS, TILE), F32),
             pltpu.VMEM((2, 2, 2, 4, BLOCK_ROWS, TILE), F32),
-            pltpu.VMEM((2, 4 * WANTED, TILE), F32),
-            pltpu.VMEM((2, 4 * WANTED, 8 * SLOTS), BF16),
+            pltpu.VMEM((2, 4 * SLOTS, TILE), F32),
+            pltpu.VMEM((2, 4 * SLOTS, 8 * SLOTS), BF16),
+            pltpu.VMEM((2, 4 * CHUNK, 8 * SLOTS), BF16),
             pltpu.VMEM((2, 8 * SLOTS, TILE), BF16),
             pltpu.VMEM((SLOTS, TILE), BF16),
             pltpu.VMEM((ROW_BLOCKS, SLOTS), BF16),
@@ -611,16 +642,16 @@
             pltpu.VMEM((2, 2, 4, CHUNK // 2, TILE), F32),
             pltpu.VMEM((2, ROW_BLOCKS + 8, TILE), F32),
             pltpu.VMEM((2, 4, ROW_BLOCKS + 8, TILE), F32),
-            pltpu.VMEM((3, 8, TILE), F32),
-            pltpu.VMEM((3, 4, 8, TILE), F32),
+            pltpu.VMEM((8, TILE), F32),
+            pltpu.VMEM((4, 4, 2, 8, TILE), F32),
             pltpu.VMEM(dense_shape, F32),
             pltpu.VMEM(dense_shape, F32),
             pltpu.VMEM(dense_shape, F32),
             dma((LOAD_CHUNKS,)),
             dma((3,)),
             dma((4,)),
-            dma((2, 2, 2, 4)),
-            dma((2, 2, 2, 4)),
+            dma((2, 2, 2, 2, 4)),
+            dma((2, 2, 2, 2, 4)),
             dma((2, 2, 4)),
             dma((2, 2, 4)),
             dma((2, 2, 4)),
@@ -629,8 +660,8 @@
             dma((2, 2, 4)),
             dma((2, 4)),
             dma((2, 4)),
-            dma((3, 4)),
-            dma((3, 4)),
+            dma((4, 4, 2)),
+            dma((4, 4, 2)),
             dma((2, 3, 2, 4)),
             dma((2, 3, 2, 4)),
         ],

time: 83.2 us -> 77.1 us (0.927)
  Pallas kernels: 77.5 us -> 71.4 us
    pallas_call x1, Pallas kernels: 77.5 us -> 71.4 us  [shards(): pl.pallas_call(lsqr_kernel, out_shape=(jax.ShapeDtypeStruct(dense_shape,...]
where the time goes in v3:
time: 77.1 us; the launch traced here: 76.9 us
  Pallas kernels  71.4 us (93%)
  local copies, waits for them, and re-layouts  4.18 us (5%)
  between operations  1.3 us (2%)
    pallas_call x1, Pallas kernels, shards(): pl.pallas_call(lsqr_kernel, out_shape=(jax.ShapeDtypeStruct(dense_shape,...  71.4 us
    unnamed x8, local copies, waits for them, and re-layouts  4.18 us

profile of v3, /device:TPU:1, one launch (start us, length us, event | category | flops | bytes accessed | tf_op | source)
XLA Modules:
  0.0 76.9 jit_solution(2273853756547196553)
XLA Ops:
  1.3 0.0 copy-start
  1.3 0.7 copy-done
  2.0 0.0 copy-start.1
  2.0 0.7 copy-done.1
  2.7 0.0 copy-start.2
  2.7 0.7 copy-done.2
  3.4 71.4 %shard_map.68 = (f32[4,4,2,128,128]{4,3,2,1,0:T(8,128)S(1)}, f32[64,128]{1,0:T(8,128)S(1)}) custom-call(s32[1,1]{1,0:T(1,128)S(6)} %copy.9.count_ref, f32[64,128]{1,0:T(8,128)S(1)} %bitcast.7, s32[2,128]{1,0:T(2,128)S(1)} %bitcast.9, s32[2,128]{1,0:T(2,128)S(1)} %bitcast.10, bf16[32768,128]{1,0:T(8,128)(2,1)} %bitcast.11), custom_call_target="tpu_custom_call" | custom-call | flops 2000000000 | bytes 12582912 | tf_op jit(solution)/shard_map/pallas_call | solution.py:616
  74.8 1.5 %copy.10 = f32[524288]{0:T(1024)} copy(f32[524288]{0:T(1024)S(1)} %bitcast.6) | data formatting | bytes 4194304
  76.3 0.6 copy.11
Async XLA Ops:
  1.3 0.8 copy-start
  2.0 0.7 copy-start.1
  2.7 0.7 copy-start.2

commit v4 on v3

--- a/solution.py
+++ b/solution.py
@@ -48,7 +48,9 @@
     rows_hbm,
     cols_hbm,
     tiles_hbm,
-    slow_hbm,
+    dense_first,
+    dense_second,
+    weights_ref,
     left_ref,
     delays_ref,
     rows_ref,
@@ -61,6 +63,7 @@
     slot_hits,
     chunk_hits,
     rhs,
+    early,
     row_pick,
     row_sum,
     cols_line,
@@ -72,12 +75,10 @@
     image_in,
     norm_out,
     norm_in,
-    dense_first,
-    dense_second,
-    slow_buf,
+    chunk_buf,
     load_sem,
     small_sem,
-    store_sem,
+    own_sem,
     gather_send,
     gather_recv,
     cols_send,
@@ -197,7 +198,7 @@
         high, low = split_parts(right)
         picked[:, pl.ds(0, TILE)] = high.astype(F32)
         picked[:, pl.ds(TILE, TILE)] = low.astype(F32)
-        half = SLOTS // GROUP // 2
+        half = SLOTS // GROUP // 4
 
         @pl.loop(0, half, unroll=8)
         def _(group):
@@ -205,7 +206,7 @@
 
         result = between()
 
-        @pl.loop(half, 2 * half, unroll=8)
+        @pl.loop(half, 4 * half, unroll=8)
         def _(group):
             forward_group(group)
 
@@ -351,9 +352,28 @@
             rhs[axis, pl.ds(row, HALF), :] = first.astype(BF16)
             rhs[axis, pl.ds(row + HALF, HALF), :] = second.astype(BF16)
 
+        def half_dot(hits, axis, off, size, part):
+            span = pl.ds(part * (4 * SLOTS), 4 * SLOTS)
+            return jnp.dot(hits[axis, pl.ds(off * size, size), span], rhs[axis, span, :], preferred_element_type=F32)
+
+        def packed(out):
+            size = out.shape[0]
+            out = out + pltpu.roll(out, TILE // 2, 1)
+            return jnp.where(low_lanes[: size // 2], out[: size // 2], out[size // 2 :])
+
+        def slot_sums(axis, off):
+            return packed(early[axis, off] + half_dot(slot_hits, axis, off, SLOTS, 1))
+
+        def chunk_part(axis, off):
+            span = pl.ds(off * CHUNK, CHUNK)
+            return packed(jnp.dot(chunk_hits[axis, span, :], rhs[axis], preferred_element_type=F32))
+
         for axis in range(2):
             for off in range(4):
                 take(axis, 0, off)
+        for axis in range(2):
+            for off in SIDES + (0,):
+                early[axis, off] = half_dot(slot_hits, axis, off, SLOTS, 0)
         for axis in range(2):
             for off in (0, 3, 1, 2):
                 block = gathered.at[step, axis, 1, off]
@@ -364,42 +384,39 @@
         line_scalars = tree4([gathered[step, 0, 0, off, pl.ds(HALF, 8), :] for off in range(4)])
         line_scalars = line_scalars + tree4([gathered[step, 0, 1, off, pl.ds(HALF, 8), :] for off in range(4)])
 
-        def wanted_sums(hits, axis, off, size):
-            out = jnp.dot(hits[axis, pl.ds(off * size, size), :], rhs[axis], preferred_element_type=F32)
-            out = out + pltpu.roll(out, TILE // 2, 1)
-            return jnp.where(low_lanes[: size // 2], out[: size // 2], out[size // 2 :])
-
-        for axis in range(2):
-            for off in SIDES + (0,):
-                sums_out[step, axis, off, pl.ds(0, HALF), :] = wanted_sums(slot_hits, axis, off, SLOTS)
+        for axis in range(2):
+            for off in SIDES:
+                sums_out[step, axis, off, pl.ds(0, HALF), :] = slot_sums(axis, off)
                 sums_out[step, axis, off, pl.ds(HALF, 8), :] = line_scalars
-                if off:
-                    slot = (step, axis, (-off) % 4)
-                    copy = remote(
-                        sums_out.at[step, axis, off],
-                        sums_in.at[slot],
-                        sums_send.at[slot],
-                        sums_recv.at[slot],
-                        line(1 - axis, off),
-                    )
-                    copy.start()
-                    sent.append(copy)
+                slot = (step, axis, (-off) % 4)
+                copy = remote(
+                    sums_out.at[step, axis, off],
+                    sums_in.at[slot],
+                    sums_send.at[slot],
+                    sums_recv.at[slot],
+                    line(1 - axis, off),
+                )
+                copy.start()
+                sent.append(copy)
         if first_step:
             mark_chunks()
         for axis in range(2):
-            for off in SIDES + (0,):
-                chunk_out[step, axis, off] = wanted_sums(chunk_hits, axis, off, CHUNK)
-                if off:
-                    slot = (step, axis, (-off) % 4)
-                    copy = remote(
-                        chunk_out.at[step, axis, off],
-                        chunk_in.at[slot],
-                        chunk_send.at[slot],
-                        chunk_recv.at[slot],
-                        line(1 - axis, off),
-                    )
-                    copy.start()
-                    sent.append(copy)
+            for off in SIDES:
+                chunk_out[step, axis, off] = chunk_part(axis, off)
+                slot = (step, axis, (-off) % 4)
+                copy = remote(
+                    chunk_out.at[step, axis, off],
+                    chunk_in.at[slot],
+                    chunk_send.at[slot],
+                    chunk_recv.at[slot],
+                    line(1 - axis, off),
+                )
+                copy.start()
+                sent.append(copy)
+        for axis in range(2):
+            sums_out[step, axis, 0, pl.ds(0, HALF), :] = slot_sums(axis, 0)
+            sums_out[step, axis, 0, pl.ds(HALF, 8), :] = line_scalars
+            chunk_out[step, axis, 0] = chunk_part(axis, 0)
         if not first_step:
             dense_three(0, dense_first, (0, 3, 1, 2))
         totals = []
@@ -423,16 +440,19 @@
         return jnp.concatenate(lane_swap(totals[0], totals[1]), axis=0)
 
     def dense_one(step, dense, chunk):
-        dense[at_x, at_z, core] = chunk
+        chunk_buf[step] = chunk
+        own = pltpu.make_async_copy(chunk_buf.at[step], dense.at[at_x, at_z, core], own_sem.at[step])
+        own.start()
         for along in range(2):
             for side in SIDES:
                 span = pl.ds(along * (CHUNK // 2), CHUNK // 2)
                 block = dense.at[at_x, at_z, core, span]
                 slot = (step, 0, along, (-side) % 4)
                 device = peer(0, side) if along else peer(side, 0)
-                copy = remote(block, block, dense_send.at[slot], dense_recv.at[slot], device)
+                copy = remote(chunk_buf.at[step, span], block, dense_send.at[slot], dense_recv.at[slot], device)
                 copy.start()
                 sent.append(copy)
+        own.wait()
 
     def dense_two(step, dense):
         for along in range(2):
@@ -594,17 +614,23 @@
 
     dense_done(0, dense_first)
     dense_done(1, dense_second)
-    stores = []
+    weights_ref[...] = scalar_rows([weight_first, weight_second])
+    for copy in sent:
+        copy.wait_send()
+
+
+def combine_kernel(first, second, weights, left, slow_hbm, left_hbm, buffer, sems):
+    copies = [pltpu.make_async_copy(left, left_hbm, sems.at[4])]
+    copies[0].start()
+    weight_first, weight_second = weights[0:1, :], weights[1:2, :]
     for off in range(4):
         for to_z in range(4):
-            slow_buf[off, to_z] = dense_first[off, to_z] * weight_first + dense_second[off, to_z] * weight_second
-        store = pltpu.make_async_copy(slow_buf.at[off], slow_hbm.at[off], store_sem.at[off])
-        store.start()
-        stores.append(store)
-    for store in stores:
-        store.wait()
-    for copy in sent:
-        copy.wait_send()
+            buffer[off, to_z] = first[off, to_z] * weight_first + second[off, to_z] * weight_second
+        copy = pltpu.make_async_copy(buffer.at[off], slow_hbm.at[off], sems.at[off])
+        copy.start()
+        copies.append(copy)
+    for copy in copies:
+        copy.wait()
 
 
 def shards(delays, kernel_tiles, row_blocks, col_blocks, tile_counts):
@@ -613,14 +639,16 @@
     hbm = pl.BlockSpec(memory_space=pltpu.HBM)
     anywhere = pl.BlockSpec(memory_space=pl.ANY)
     dense_shape = (4, 4, 2, CHUNK, TILE)
-    slowness, left = pl.pallas_call(
+    first, second, weights, left = pl.pallas_call(
         lsqr_kernel,
         out_shape=(
             jax.ShapeDtypeStruct(dense_shape, F32),
+            jax.ShapeDtypeStruct(dense_shape, F32),
+            jax.ShapeDtypeStruct((8, TILE), F32),
             jax.ShapeDtypeStruct((ROW_BLOCKS, TILE), F32),
         ),
         in_specs=[pl.BlockSpec(memory_space=pltpu.SMEM)] + [hbm] * 4,
-        out_specs=(anywhere, vmem),
+        out_specs=(anywhere, anywhere, vmem, vmem),
         scratch_shapes=[
             pltpu.VMEM((ROW_BLOCKS, TILE), F32),
             pltpu.VMEM((2, HALF), jnp.int32),
@@ -633,6 +661,7 @@
             pltpu.VMEM((2, 4 * SLOTS, 8 * SLOTS), BF16),
             pltpu.VMEM((2, 4 * CHUNK, 8 * SLOTS), BF16),
             pltpu.VMEM((2, 8 * SLOTS, TILE), BF16),
+            pltpu.VMEM((2, 4, SLOTS, TILE), F32),
             pltpu.VMEM((SLOTS, TILE), BF16),
             pltpu.VMEM((ROW_BLOCKS, SLOTS), BF16),
             pltpu.VMEM((2, 2, 4, 8, TILE), F32),
@@ -644,12 +673,10 @@
             pltpu.VMEM((2, 4, ROW_BLOCKS + 8, TILE), F32),
             pltpu.VMEM((8, TILE), F32),
             pltpu.VMEM((4, 4, 2, 8, TILE), F32),
-            pltpu.VMEM(dense_shape, F32),
-            pltpu.VMEM(dense_shape, F32),
-            pltpu.VMEM(dense_shape, F32),
+            pltpu.VMEM((2, CHUNK, TILE), F32),
             dma((LOAD_CHUNKS,)),
             dma((3,)),
-            dma((4,)),
+            dma((2,)),
             dma((2, 2, 2, 2, 4)),
             dma((2, 2, 2, 2, 4)),
             dma((2, 2, 4)),
@@ -676,6 +703,18 @@
         col_blocks.reshape(2, HALF),
         kernel_tiles.reshape(SLOTS * TILE, TILE),
     )
+    slowness, left = pl.pallas_call(
+        combine_kernel,
+        out_shape=(
+            jax.ShapeDtypeStruct(dense_shape, F32),
+            jax.ShapeDtypeStruct((ROW_BLOCKS, TILE), F32),
+        ),
+        in_specs=[vmem] * 4,
+        out_specs=(anywhere, anywhere),
+        scratch_shapes=[pltpu.VMEM(dense_shape, F32), dma((5,))],
+        compiler_params=pltpu.CompilerParams(vmem_limit_bytes=8 * 2**20),
+        cost_estimate=pl.CostEstimate(flops=2**20, bytes_accessed=6 * 2**20, transcendentals=0),
+    )(first, second, weights, left)
     return slowness.reshape(-1), left.reshape(-1)
 
 

time: 77.1 us -> 71.8 us (0.931)
  Pallas kernels: 71.4 us -> 68 us
  local copies, waits for them, and re-layouts: 4.18 us -> 2.11 us
    pallas_call x1, Pallas kernels: 71.4 us -> 66.6 us  [shards(): pl.pallas_call(lsqr_kernel, out_shape=(jax.ShapeDtypeStruct(dense_shape,...]
    unnamed x8 -> x6, local copies, waits for them, and re-layouts: 4.18 us -> 2.11 us
    pallas_call x0 -> x1, Pallas kernels: none -> 1.41 us  [shards(): pl.pallas_call(combine_kernel, out_shape=(jax.ShapeDtypeStruct(dense_shap...]
where the time goes in v4:
time: 71.8 us; the launch traced here: 71.6 us
  Pallas kernels  68 us (95%)
  local copies, waits for them, and re-layouts  2.11 us (3%)
  between operations  1.46 us (2%)
    pallas_call x1, Pallas kernels, shards(): pl.pallas_call(lsqr_kernel, out_shape=(jax.ShapeDtypeStruct(dense_shape,...  66.6 us
    unnamed x6, local copies, waits for them, and re-layouts  2.11 us

profile of v4, /device:TPU:1, one launch (start us, length us, event | category | flops | bytes accessed | tf_op | source)
XLA Modules:
  0.0 71.6 jit_solution(6846748175525766861)
XLA Ops:
  1.3 0.0 copy-start
  1.3 0.7 %copy-done = f32[8192]{0:T(1024)S(1)} copy-done((f32[8192]{0:T(1024)S(1)}, f32[8192]{0:T(1024)}, u32[]{:S(2)}) %copy-start) | copy-done | bytes 32792
  2.0 0.0 copy-start.1
  2.0 0.7 copy-done.1
  2.7 0.0 copy-start.2
  2.7 0.7 copy-done.2
  3.4 66.6 %shard_map.68 = (f32[4,4,2,128,128]{4,3,2,1,0:T(8,128)S(1)}, f32[4,4,2,128,128]{4,3,2,1,0:T(8,128)S(1)}, f32[8,128]{1,0:T(8,128)S(1)}, f32[64,128]{1,0:T(8,128)S(1)}) custom-call(s32[1,1]{1,0:T(1,128)S(6)} %copy.7.count_ref, f32[64,128]{1,0:T(8,128)S(1)} %bitcast.6, s32[2,128]{1,0:T(2,128)S(1)} %bitcast.7, s32[2,128]{1,0:T(2,128)S(1)} %bitcast.8, ...), custom_call_target="tpu_custom_call" | custom-call | flops 2000000000 | bytes 12582912 | tf_op jit(solution)/shard_map/pallas_call | solution.py:642
  70.0 1.4 %shard_map.69 = (f32[4,4,2,128,128]{4,3,2,1,0:T(8,128)}, f32[64,128]{1,0:T(8,128)}) custom-call(f32[4,4,2,128,128]{4,3,2,1,0:T(8,128)S(1)} %get-tuple-element.8.first, f32[4,4,2,128,128]{4,3,2,1,0:T(8,128)S(1)} %get-tuple-element.9.second, f32[8,128]{1,0:T(8,128)S(1)} %get-tuple-element.10.weights, f32[64,128]{1,0:T(8,128)S(1)} %get-tuple-element.11.left), custom_call_target="tpu_custom_call" | custom-call | flops 1048576 | bytes 6291456 | tf_op jit(solution)/shard_map/pallas_call | solution.py:706
Async XLA Ops:
  1.3 0.8 %copy-start = (f32[8192]{0:T(1024)S(1)}, f32[8192]{0:T(1024)}, u32[]{:S(2)}) copy-start(f32[8192]{0:T(1024)} %param.5) | copy-start | bytes 98308
  2.0 0.7 copy-start.1
  2.7 0.7 copy-start.2

commit v5 on v4

--- a/solution.py
+++ b/solution.py
@@ -64,6 +64,7 @@
     chunk_hits,
     rhs,
     early,
+    early_chunk,
     row_pick,
     row_sum,
     cols_line,
@@ -365,8 +366,9 @@
             return packed(early[axis, off] + half_dot(slot_hits, axis, off, SLOTS, 1))
 
         def chunk_part(axis, off):
-            span = pl.ds(off * CHUNK, CHUNK)
-            return packed(jnp.dot(chunk_hits[axis, span, :], rhs[axis], preferred_element_type=F32))
+            if first_step:
+                return packed(half_dot(chunk_hits, axis, off, CHUNK, 0) + half_dot(chunk_hits, axis, off, CHUNK, 1))
+            return packed(early_chunk[axis, off] + half_dot(chunk_hits, axis, off, CHUNK, 1))
 
         for axis in range(2):
             for off in range(4):
@@ -374,6 +376,10 @@
         for axis in range(2):
             for off in SIDES + (0,):
                 early[axis, off] = half_dot(slot_hits, axis, off, SLOTS, 0)
+        if not first_step:
+            for axis in range(2):
+                for off in SIDES + (0,):
+                    early_chunk[axis, off] = half_dot(chunk_hits, axis, off, CHUNK, 0)
         for axis in range(2):
             for off in (0, 3, 1, 2):
                 block = gathered.at[step, axis, 1, off]
@@ -662,6 +668,7 @@
             pltpu.VMEM((2, 4 * CHUNK, 8 * SLOTS), BF16),
             pltpu.VMEM((2, 8 * SLOTS, TILE), BF16),
             pltpu.VMEM((2, 4, SLOTS, TILE), F32),
+            pltpu.VMEM((2, 4, CHUNK, TILE), F32),
             pltpu.VMEM((SLOTS, TILE), BF16),
             pltpu.VMEM((ROW_BLOCKS, SLOTS), BF16),
             pltpu.VMEM((2, 2, 4, 8, TILE), F32),

time: 71.8 us -> 71.3 us (level)
  no operation moved by 1% of the time
where the time goes in v5:
time: 71.3 us; the launch traced here: 71 us
  Pallas kernels  67.5 us (95%)
  local copies, waits for them, and re-layouts  2.11 us (3%)
  between operations  1.46 us (2%)
    pallas_call x1, Pallas kernels, shards(): pl.pallas_call(lsqr_kernel, out_shape=(jax.ShapeDtypeStruct(dense_shape,...  66.1 us
    unnamed x6, local copies, waits for them, and re-layouts  2.11 us

profile of v5, /device:TPU:1, one launch (start us, length us, event | category | flops | bytes accessed | tf_op | source)
XLA Modules:
  0.0 71.0 jit_solution(11445409928428625419)
XLA Ops:
  1.3 0.0 copy-start
  1.3 0.7 %copy-done = f32[8192]{0:T(1024)S(1)} copy-done((f32[8192]{0:T(1024)S(1)}, f32[8192]{0:T(1024)}, u32[]{:S(2)}) %copy-start) | copy-done | bytes 32792
  2.0 0.0 copy-start.1
  2.0 0.7 copy-done.1
  2.7 0.0 copy-start.2
  2.7 0.7 copy-done.2
  3.4 66.1 %shard_map.68 = (f32[4,4,2,128,128]{4,3,2,1,0:T(8,128)S(1)}, f32[4,4,2,128,128]{4,3,2,1,0:T(8,128)S(1)}, f32[8,128]{1,0:T(8,128)S(1)}, f32[64,128]{1,0:T(8,128)S(1)}) custom-call(s32[1,1]{1,0:T(1,128)S(6)} %copy.7.count_ref, f32[64,128]{1,0:T(8,128)S(1)} %bitcast.6, s32[2,128]{1,0:T(2,128)S(1)} %bitcast.7, s32[2,128]{1,0:T(2,128)S(1)} %bitcast.8, ...), custom_call_target="tpu_custom_call" | custom-call | flops 2000000000 | bytes 12582912 | tf_op jit(solution)/shard_map/pallas_call | solution.py:648
  69.5 1.4 %shard_map.69 = (f32[4,4,2,128,128]{4,3,2,1,0:T(8,128)}, f32[64,128]{1,0:T(8,128)}) custom-call(f32[4,4,2,128,128]{4,3,2,1,0:T(8,128)S(1)} %get-tuple-element.8.first, f32[4,4,2,128,128]{4,3,2,1,0:T(8,128)S(1)} %get-tuple-element.9.second, f32[8,128]{1,0:T(8,128)S(1)} %get-tuple-element.10.weights, f32[64,128]{1,0:T(8,128)S(1)} %get-tuple-element.11.left), custom_call_target="tpu_custom_call" | custom-call | flops 1048576 | bytes 6291456 | tf_op jit(solution)/shard_map/pallas_call | solution.py:713
Async XLA Ops:
  1.3 0.8 %copy-start = (f32[8192]{0:T(1024)S(1)}, f32[8192]{0:T(1024)}, u32[]{:S(2)}) copy-start(f32[8192]{0:T(1024)} %param.5) | copy-start | bytes 98308
  2.0 0.7 copy-start.1
  2.7 0.7 copy-start.2

commit v6 on v5

--- a/solution.py
+++ b/solution.py
@@ -195,19 +195,19 @@
             chosen = jnp.where(sub_group == slot, out[:, slot * TILE : (slot + 1) * TILE], chosen)
         slot_products[pl.ds(group * GROUP, GROUP), :] = chosen
 
-    def forward(right, between):
+    def forward(right, between, cut):
         high, low = split_parts(right)
         picked[:, pl.ds(0, TILE)] = high.astype(F32)
         picked[:, pl.ds(TILE, TILE)] = low.astype(F32)
-        half = SLOTS // GROUP // 4
-
-        @pl.loop(0, half, unroll=8)
+        groups = SLOTS // GROUP
+
+        @pl.loop(0, cut, unroll=4)
         def _(group):
             forward_group(group)
 
         result = between()
 
-        @pl.loop(half, 4 * half, unroll=8)
+        @pl.loop(cut, groups, unroll=4)
         def _(group):
             forward_group(group)
 
@@ -537,6 +537,8 @@
     def norm_sum(scalars, between):
         value = scalar_rows(scalars)
         norm_out[...] = value
+        earlier = list(sent)
+        sent.clear()
         offs = [(x, z, c) for x in (2, 1, 3, 0) for z in (2, 1, 3, 0) for c in (1, 0) if (x, z, c) != (0, 0, 0)]
         for x, z, c in offs:
             slot = ((-x) % 4, (-z) % 4, c)
@@ -544,6 +546,8 @@
             copy.start()
             sent.append(copy)
         between()
+        for copy in earlier:
+            copy.wait_send()
         for slot in offs:
             block = norm_in.at[slot]
             remote(block, block, norm_send.at[slot], norm_recv.at[slot], sibling).wait_recv()
@@ -569,7 +573,7 @@
         dense_one(0, dense_first, chunk)
         return chunk
 
-    image, chunk_first = forward(right_first, finish_first)
+    image, chunk_first = forward(right_first, finish_first, 8)
     image_start(0, image, [total_of(chunk_first * chunk_first)])
     dense_two(0, dense_first)
     image, scalars = image_finish(0)
@@ -593,7 +597,7 @@
         dense_one(1, dense_second, chunk)
         return chunk
 
-    image, chunk_second = forward(second_right(sums, right_first), finish_second)
+    image, chunk_second = forward(second_right(sums, right_first), finish_second, 4)
     image_start(1, image, [total_of(chunk_second * chunk_second)])
     dense_two(1, dense_second)
     image, scalars = image_finish(1)

time: 71.3 us -> 71.3 us (level)
  no operation moved by 1% of the time
where the time goes in v6:
time: 71.3 us; the launch traced here: 71.1 us
  Pallas kernels  67.5 us (95%)
  local copies, waits for them, and re-layouts  2.11 us (3%)
  between operations  1.46 us (2%)
    pallas_call x1, Pallas kernels, shards(): pl.pallas_call(lsqr_kernel, out_shape=(jax.ShapeDtypeStruct(dense_shape,...  66.1 us
    unnamed x6, local copies, waits for them, and re-layouts  2.11 us

profile of v6, /device:TPU:1, one launch (start us, length us, event | category | flops | bytes accessed | tf_op | source)
XLA Modules:
  0.0 71.1 jit_solution(9176177568252965429)
XLA Ops:
  1.3 0.0 copy-start
  1.3 0.7 %copy-done = f32[8192]{0:T(1024)S(1)} copy-done((f32[8192]{0:T(1024)S(1)}, f32[8192]{0:T(1024)}, u32[]{:S(2)}) %copy-start) | copy-done | bytes 32792
  2.0 0.0 copy-start.1
  2.0 0.7 copy-done.1
  2.7 0.0 copy-start.2
  2.7 0.7 copy-done.2
  3.4 66.1 %shard_map.68 = (f32[4,4,2,128,128]{4,3,2,1,0:T(8,128)S(1)}, f32[4,4,2,128,128]{4,3,2,1,0:T(8,128)S(1)}, f32[8,128]{1,0:T(8,128)S(1)}, f32[64,128]{1,0:T(8,128)S(1)}) custom-call(s32[1,1]{1,0:T(1,128)S(6)} %copy.7.count_ref, f32[64,128]{1,0:T(8,128)S(1)} %bitcast.6, s32[2,128]{1,0:T(2,128)S(1)} %bitcast.7, s32[2,128]{1,0:T(2,128)S(1)} %bitcast.8, ...), custom_call_target="tpu_custom_call" | custom-call | flops 2000000000 | bytes 12582912 | tf_op jit(solution)/shard_map/pallas_call | solution.py:652
  69.5 1.4 %shard_map.69 = (f32[4,4,2,128,128]{4,3,2,1,0:T(8,128)}, f32[64,128]{1,0:T(8,128)}) custom-call(f32[4,4,2,128,128]{4,3,2,1,0:T(8,128)S(1)} %get-tuple-element.8.first, f32[4,4,2,128,128]{4,3,2,1,0:T(8,128)S(1)} %get-tuple-element.9.second, f32[8,128]{1,0:T(8,128)S(1)} %get-tuple-element.10.weights, f32[64,128]{1,0:T(8,128)S(1)} %get-tuple-element.11.left), custom_call_target="tpu_custom_call" | custom-call | flops 1048576 | bytes 6291456 | tf_op jit(solution)/shard_map/pallas_call | solution.py:717
Async XLA Ops:
  1.3 0.8 %copy-start = (f32[8192]{0:T(1024)S(1)}, f32[8192]{0:T(1024)}, u32[]{:S(2)}) copy-start(f32[8192]{0:T(1024)} %param.5) | copy-start | bytes 98308
  2.0 0.7 copy-start.1
  2.7 0.7 copy-start.2
